TPU v7x, 32 devices: a whole 2x2x4 slice. The times are simulated.
32 devices in a mesh: wide: 8 (over z, y), narrow: 4 (over x, core).
Axes of the slice: x: 2, y: 2, z: 4, core: 2. Of those that a mesh axis runs over, the one named last changes fastest.
Arguments:
- tokens: bfloat16 [32, 1024, 768], P(('wide', 'narrow')), may hold values from -6 to 6
- first_values: bfloat16 [32, 1024, 384], P(('wide', 'narrow')), may hold values from -6 to 6
- cotangent: bfloat16 [32, 1024, 768], P(('wide', 'narrow')), may hold values from -6 to 6
- lengths: int32 [32], P(('wide', 'narrow')), may hold values from 1 to 1024, 16384 in all
- weight_in: float32 [768, 1920], P(('wide', 'narrow')), may hold values from -0.21875 to 0.21875
- weight_out: float32 [768, 768], P(('wide', 'narrow')), may hold values from -1.75 to 1.75
- weight_up: float32 [768, 3072], P(('wide', 'narrow')), may hold values from -0.21875 to 0.21875
- weight_down: float32 [3072, 768], P(('wide', 'narrow')), may hold values from -0.109375 to 0.109375
- first_in: float32 [768, 1920], P(('wide', 'narrow')), may hold values from -0.0015348548 to 0.0015348548
- first_out: float32 [768, 768], P(('wide', 'narrow')), may hold values from -0.0015348548 to 0.0015348548
- first_up: float32 [768, 3072], P(('wide', 'narrow')), may hold values from -0.0015348548 to 0.0015348548
- first_down: float32 [3072, 768], P(('wide', 'narrow')), may hold values from -0.0015348548 to 0.0015348548
- second_in: float32 [768, 1920], P(('wide', 'narrow')), may hold values from 1.472362e-07 to 5.889448e-07
- second_out: float32 [768, 768], P(('wide', 'narrow')), may hold values from 1.472362e-07 to 5.889448e-07
- second_up: float32 [768, 3072], P(('wide', 'narrow')), may hold values from 1.472362e-07 to 5.889448e-07
- second_down: float32 [3072, 768], P(('wide', 'narrow')), may hold values from 1.472362e-07 to 5.889448e-07
- shadow_in: float32 [768, 1920], P(('wide', 'narrow')), may hold values from -0.21875 to 0.21875
- shadow_out: float32 [768, 768], P(('wide', 'narrow')), may hold values from -1.75 to 1.75
- shadow_up: float32 [768, 3072], P(('wide', 'narrow')), may hold values from -0.21875 to 0.21875
- shadow_down: float32 [3072, 768], P(('wide', 'narrow')), may hold values from -0.109375 to 0.109375
- vectors: float32 [8832], replicated, as said below
- first_vectors: float32 [8832], replicated, may hold values from -0.006139419 to 0.006139419
- second_vectors: float32 [8832], replicated, may hold values from 2.355779e-06 to 9.423116e-06
- shadow_vectors: float32 [8832], replicated, may hold values from 0.5 to 1.5
Outputs:
- result: bfloat16 [32, 1024, 768], P(('wide', 'narrow'))
- grad_tokens: bfloat16 [32, 1024, 768], P(('wide', 'narrow'))
- grad_values: bfloat16 [32, 1024, 384], P(('wide', 'narrow'))
- grad_norm: float32 [], replicated
- updated_in: float32 [768, 1920], P(('wide', 'narrow'))
- moment_in: float32 [768, 1920], P(('wide', 'narrow'))
- square_in: float32 [768, 1920], P(('wide', 'narrow'))
- average_in: float32 [768, 1920], P(('wide', 'narrow'))
- updated_out: float32 [768, 768], P(('wide', 'narrow'))
- moment_out: float32 [768, 768], P(('wide', 'narrow'))
- square_out: float32 [768, 768], P(('wide', 'narrow'))
- average_out: float32 [768, 768], P(('wide', 'narrow'))
- updated_up: float32 [768, 3072], P(('wide', 'narrow'))
- moment_up: float32 [768, 3072], P(('wide', 'narrow'))
- square_up: float32 [768, 3072], P(('wide', 'narrow'))
- average_up: float32 [768, 3072], P(('wide', 'narrow'))
- updated_down: float32 [3072, 768], P(('wide', 'narrow'))
- moment_down: float32 [3072, 768], P(('wide', 'narrow'))
- square_down: float32 [3072, 768], P(('wide', 'narrow'))
- average_down: float32 [3072, 768], P(('wide', 'narrow'))
- updated_vectors: float32 [8832], replicated
- moment_vectors: float32 [8832], replicated
- square_vectors: float32 [8832], replicated
- average_vectors: float32 [8832], replicated
Inputs may be any that keep to these rules, and one draw needn't show every extreme that they name: `lengths`: the longest sequence has exactly 1024 real tokens; positions from a sequence's length on are padding. `vectors`: laid end to end: first norm's gain and shift, second norm's gain and shift, query bias, fresh value bias, output projection bias, hidden bias, down projection bias.
All inputs are finite; a program needn't handle non-finite values. No bound on the sum of `lengths` on one device may be relied on, other than what follows from the above.
Results may differ from a plain program's by a relative error of at most 0.013.
The roundings to bfloat16 on the way count: a program that leaves them out, or rounds other values in their place, can miss the bound.
Values may be sent and summed in bfloat16 or wider, within the bound.
A program may use at most 256 MiB of HBM per device.

v0:
```python
import jax
import jax.numpy as jnp
from jax import lax
from jax.sharding import PartitionSpec as P

D = 768
H = 12
HD = 64
FF = 3072
VH = 6
STEP = 7


BETA_ONE = 0.5
BETA_TWO = 0.5
SHADOW_RATE = 0.5
RATE_MATRIX = 0.03
RATE_OUTPUT = 0.15
RATE_VECTOR = 0.3
DECAY_MATRIX = 0.1
CLIP = 1.0
EPS_ADAM = 1e-08
SCORE_SCALE = 0.125


def norm_rows(values, gain, shift):
    center = values - jnp.mean(values, axis=-1, keepdims=True)
    spread = jnp.mean(center * center, axis=-1, keepdims=True)
    return center * lax.rsqrt(spread + 1e-05) * gain + shift


def split_vector(vector):
    extents = [D, D, D, D, H * HD, VH * HD, D, FF, D]
    pieces = []
    offset = 0
    for extent in extents:
        pieces.append(vector[offset : offset + extent])
        offset += extent
    return pieces


def gather_copies(lowered):
    return (
        lax.all_gather(lowered[0], ("wide", "narrow"), axis=0, tiled=True),
        lax.all_gather(lowered[1], ("wide", "narrow"), axis=0, tiled=True),
        lax.all_gather(lowered[2], ("wide", "narrow"), axis=0, tiled=True),
        lax.all_gather(lowered[3], ("wide", "narrow"), axis=0, tiled=True),
    )


def sum_gradients(partials):
    return (
        lax.psum_scatter(partials[0], ("wide", "narrow"), scatter_dimension=0, tiled=True),
        lax.psum_scatter(partials[1], ("wide", "narrow"), scatter_dimension=0, tiled=True),
        lax.psum_scatter(partials[2], ("wide", "narrow"), scatter_dimension=0, tiled=True),
        lax.psum_scatter(partials[3], ("wide", "narrow"), scatter_dimension=0, tiled=True),
    )


def adam_step(master, grad, first, second, shadow, rate, decay):
    moment = BETA_ONE * first + (1.0 - BETA_ONE) * grad
    square = BETA_TWO * second + (1.0 - BETA_TWO) * grad * grad
    moment_hat = moment / (1.0 - BETA_ONE**STEP)
    square_hat = square / (1.0 - BETA_TWO**STEP)
    updated = master - rate * (moment_hat / (jnp.sqrt(square_hat) + EPS_ADAM) + decay * master)
    average = SHADOW_RATE * shadow + (1.0 - SHADOW_RATE) * updated
    return (updated, moment, square, average)


def body(
    tokens,
    first_values,
    cotangent,
    lengths,
    weight_in,
    weight_out,
    weight_up,
    weight_down,
    first_in,
    first_out,
    first_up,
    first_down,
    second_in,
    second_out,
    second_up,
    second_down,
    shadow_in,
    shadow_out,
    shadow_up,
    shadow_down,
    vectors,
    first_vectors,
    second_vectors,
    shadow_vectors,
):
    masters = (weight_in, weight_out, weight_up, weight_down)
    lowered = tuple((master.astype(jnp.bfloat16) for master in masters))
    copies = gather_copies(lowered)
    slot_count, seq_len = (tokens.shape[0], tokens.shape[1])
    row_count = slot_count * seq_len
    span = H * HD
    (
        gain_one,
        shift_one,
        gain_two,
        shift_two,
        bias_query,
        bias_value,
        bias_out,
        bias_up,
        bias_down,
    ) = split_vector(vectors)
    positions = jnp.arange(seq_len, dtype=jnp.int32)
    valid = (positions[None, :] < lengths[:, None]).astype(jnp.float32).reshape(row_count, 1)
    inputs = tokens.astype(jnp.float32).reshape(row_count, D)
    normed = norm_rows(inputs, gain_one, shift_one)
    normed_low = normed.astype(jnp.bfloat16)
    project = jnp.dot(normed_low, copies[0], preferred_element_type=jnp.float32)
    query_low = (project[:, :span] + bias_query).astype(jnp.bfloat16)
    key_low = project[:, span : 2 * span].astype(jnp.bfloat16)
    fresh_low = (project[:, 2 * span :] + bias_value).astype(jnp.bfloat16)
    query_heads = query_low.reshape(slot_count, seq_len, H, HD)
    key_heads = key_low.reshape(slot_count, seq_len, H, HD)
    value_heads = jnp.concatenate(
        [
            fresh_low.reshape(slot_count, seq_len, VH, HD),
            first_values.reshape(slot_count, seq_len, H - VH, HD),
        ],
        axis=2,
    )
    block = min(512, seq_len)
    per_slot = seq_len // block
    block_ids = jnp.arange(slot_count * per_slot, dtype=jnp.int32)

    def masked_scores(index):
        slot = index // per_slot
        offset = index % per_slot * block
        query_block = lax.dynamic_slice_in_dim(
            lax.dynamic_index_in_dim(query_heads, slot, 0, False), offset, block, 0
        )
        key_slot = lax.dynamic_index_in_dim(key_heads, slot, 0, False)
        value_slot = lax.dynamic_index_in_dim(value_heads, slot, 0, False)
        raw = (
            jnp.einsum("qhe,khe->hqk", query_block, key_slot, preferred_element_type=jnp.float32)
            * SCORE_SCALE
        )
        row_pos = offset + jnp.arange(block, dtype=jnp.int32)
        column_pos = jnp.arange(seq_len, dtype=jnp.int32)
        length = lax.dynamic_index_in_dim(lengths, slot, 0, False)
        allowed = (column_pos[None, :] <= row_pos[:, None]) & (column_pos[None, :] < length)
        return (
            jnp.where(allowed[None], raw, -1000000000.0),
            slot,
            offset,
            query_block,
            key_slot,
            value_slot,
        )

    def forward_block(index):
        scores, slot, offset, query_block, key_slot, value_slot = masked_scores(index)
        highest = jnp.max(scores, axis=-1, keepdims=True)
        exponent = jnp.exp(scores - highest)
        summed = jnp.sum(exponent, axis=-1, keepdims=True)
        probs_low = (exponent / summed).astype(jnp.bfloat16)
        block_out = jnp.einsum(
            "hqk,khe->qhe", probs_low, value_slot, preferred_element_type=jnp.float32
        )
        return (block_out, (highest + jnp.log(summed))[..., 0])

    attended, log_totals = lax.map(forward_block, block_ids)
    attended_low = attended.reshape(row_count, span).astype(jnp.bfloat16)
    branch = jnp.dot(attended_low, copies[1], preferred_element_type=jnp.float32) + bias_out
    middle = inputs + branch
    normed_two = norm_rows(middle, gain_two, shift_two)
    normed_two_low = normed_two.astype(jnp.bfloat16)
    hidden_pre = jnp.dot(normed_two_low, copies[2], preferred_element_type=jnp.float32) + bias_up
    active_low = jax.nn.gelu(hidden_pre, approximate=True).astype(jnp.bfloat16)
    feed = jnp.dot(active_low, copies[3], preferred_element_type=jnp.float32) + bias_down
    result = (valid * (middle + feed)).astype(jnp.bfloat16).reshape(slot_count, seq_len, D)
    back_copies = gather_copies(lowered)
    grad_out = cotangent.astype(jnp.float32).reshape(row_count, D) * valid
    grad_out_low = grad_out.astype(jnp.bfloat16)
    grad_down = jnp.einsum(
        "nf,nd->fd", active_low, grad_out_low, preferred_element_type=jnp.float32
    )
    grad_bias_down = jnp.sum(grad_out, axis=0)
    grad_active = jnp.einsum(
        "nd,fd->nf", grad_out_low, back_copies[3], preferred_element_type=jnp.float32
    )
    unused, gelu_back = jax.vjp(lambda values: jax.nn.gelu(values, approximate=True), hidden_pre)
    grad_hidden_low = gelu_back(grad_active)[0].astype(jnp.bfloat16)
    grad_up = jnp.einsum(
        "nd,nf->df", normed_two_low, grad_hidden_low, preferred_element_type=jnp.float32
    )
    grad_bias_up = jnp.sum(grad_hidden_low.astype(jnp.float32), axis=0)
    grad_normed_two = jnp.einsum(
        "nf,df->nd", grad_hidden_low, back_copies[2], preferred_element_type=jnp.float32
    )
    unused, norm_two_back = jax.vjp(norm_rows, middle, gain_two, shift_two)
    grad_middle_norm, grad_gain_two, grad_shift_two = norm_two_back(grad_normed_two)
    grad_middle = grad_out + grad_middle_norm
    grad_branch_low = grad_middle.astype(jnp.bfloat16)
    grad_weight_out = jnp.einsum(
        "ne,nd->ed", attended_low, grad_branch_low, preferred_element_type=jnp.float32
    )
    grad_bias_out = jnp.sum(grad_branch_low.astype(jnp.float32), axis=0)
    grad_attended_low = jnp.einsum(
        "nd,ed->ne", grad_branch_low, back_copies[1], preferred_element_type=jnp.float32
    ).astype(jnp.bfloat16)
    grad_heads = grad_attended_low.reshape(slot_count, seq_len, H, HD)

    def backward_block(index):
        scores, slot, offset, query_block, key_slot, value_slot = masked_scores(index)
        grad_block = lax.dynamic_slice_in_dim(
            lax.dynamic_index_in_dim(grad_heads, slot, 0, False), offset, block, 0
        )
        log_block = lax.dynamic_index_in_dim(log_totals, index, 0, False)
        probs = jnp.exp(scores - log_block[..., None])
        probs_low = probs.astype(jnp.bfloat16)
        grad_probs = jnp.einsum(
            "qhe,khe->hqk", grad_block, value_slot, preferred_element_type=jnp.float32
        )
        inner = jnp.sum(probs * grad_probs, axis=-1, keepdims=True)
        grad_scores = (probs * (grad_probs - inner)).astype(jnp.bfloat16)
        grad_query = (
            jnp.einsum("hqk,khe->qhe", grad_scores, key_slot, preferred_element_type=jnp.float32)
            * SCORE_SCALE
        )
        grad_key = (
            jnp.einsum("hqk,qhe->khe", grad_scores, query_block, preferred_element_type=jnp.float32)
            * SCORE_SCALE
        )
        grad_value = jnp.einsum(
            "hqk,qhe->khe", probs_low, grad_block, preferred_element_type=jnp.float32
        )
        return (grad_query, grad_key, grad_value)

    grad_query, grad_key, grad_value = lax.map(backward_block, block_ids)
    grad_query_low = grad_query.reshape(row_count, span).astype(jnp.bfloat16)
    grad_key_low = (
        grad_key.reshape(slot_count, per_slot, seq_len, H, HD)
        .sum(axis=1)
        .reshape(row_count, span)
        .astype(jnp.bfloat16)
    )
    grad_value_all = grad_value.reshape(slot_count, per_slot, seq_len, H, HD).sum(axis=1)
    grad_fresh_low = grad_value_all[:, :, :VH].reshape(row_count, VH * HD).astype(jnp.bfloat16)
    grad_values = (
        grad_value_all[:, :, VH:].reshape(slot_count, seq_len, (H - VH) * HD).astype(jnp.bfloat16)
    )
    grad_bias_query = jnp.sum(grad_query_low.astype(jnp.float32), axis=0)
    grad_bias_value = jnp.sum(grad_fresh_low.astype(jnp.float32), axis=0)
    grad_project = jnp.concatenate([grad_query_low, grad_key_low, grad_fresh_low], axis=1)
    grad_weight_in = jnp.einsum(
        "nd,ne->de", normed_low, grad_project, preferred_element_type=jnp.float32
    )
    grad_normed = jnp.einsum(
        "ne,de->nd", grad_project, back_copies[0], preferred_element_type=jnp.float32
    )
    unused, norm_one_back = jax.vjp(norm_rows, inputs, gain_one, shift_one)
    grad_inputs_norm, grad_gain_one, grad_shift_one = norm_one_back(grad_normed)
    grad_tokens = (
        (grad_middle + grad_inputs_norm).astype(jnp.bfloat16).reshape(slot_count, seq_len, D)
    )
    shards = sum_gradients((grad_weight_in, grad_weight_out, grad_up, grad_down))
    local_squares = jnp.float32(0.0)
    for shard in shards:
        local_squares = local_squares + jnp.sum(shard * shard)
    vector_partial = jnp.concatenate(
        [
            grad_gain_one,
            grad_shift_one,
            grad_gain_two,
            grad_shift_two,
            grad_bias_query,
            grad_bias_value,
            grad_bias_out,
            grad_bias_up,
            grad_bias_down,
        ]
    )
    vector_grad, matrix_squares = lax.psum((vector_partial, local_squares), ("wide", "narrow"))
    grad_norm = jnp.sqrt(matrix_squares + jnp.sum(vector_grad * vector_grad))
    factor = jnp.minimum(1.0, CLIP / grad_norm)
    firsts = (first_in, first_out, first_up, first_down)
    seconds = (second_in, second_out, second_up, second_down)
    shadows = (shadow_in, shadow_out, shadow_up, shadow_down)
    rates = (RATE_MATRIX, RATE_OUTPUT, RATE_MATRIX, RATE_MATRIX)
    outputs = [result, grad_tokens, grad_values, grad_norm]
    for index in range(4):
        outputs.extend(
            adam_step(
                masters[index],
                factor * shards[index],
                firsts[index],
                seconds[index],
                shadows[index],
                rates[index],
                DECAY_MATRIX,
            )
        )
    outputs.extend(
        adam_step(
            vectors,
            factor * vector_grad,
            first_vectors,
            second_vectors,
            shadow_vectors,
            RATE_VECTOR,
            0.0,
        )
    )
    return tuple(outputs)


def solution(mesh):
    return jax.shard_map(
        body,
        mesh=mesh,
        in_specs=(
            P(("wide", "narrow"), None, None),
            P(("wide", "narrow"), None, None),
            P(("wide", "narrow"), None, None),
            P(("wide", "narrow")),
            P(("wide", "narrow"), None),
            P(("wide", "narrow"), None),
            P(("wide", "narrow"), None),
            P(("wide", "narrow"), None),
            P(("wide", "narrow"), None),
            P(("wide", "narrow"), None),
            P(("wide", "narrow"), None),
            P(("wide", "narrow"), None),
            P(("wide", "narrow"), None),
            P(("wide", "narrow"), None),
            P(("wide", "narrow"), None),
            P(("wide", "narrow"), None),
            P(("wide", "narrow"), None),
            P(("wide", "narrow"), None),
            P(("wide", "narrow"), None),
            P(("wide", "narrow"), None),
            P(),
            P(),
            P(),
            P(),
        ),
        out_specs=(
            P(("wide", "narrow"), None, None),
            P(("wide", "narrow"), None, None),
            P(("wide", "narrow"), None, None),
            P(),
            P(("wide", "narrow"), None),
            P(("wide", "narrow"), None),
            P(("wide", "narrow"), None),
            P(("wide", "narrow"), None),
            P(("wide", "narrow"), None),
            P(("wide", "narrow"), None),
            P(("wide", "narrow"), None),
            P(("wide", "narrow"), None),
            P(("wide", "narrow"), None),
            P(("wide", "narrow"), None),
            P(("wide", "narrow"), None),
            P(("wide", "narrow"), None),
            P(("wide", "narrow"), None),
            P(("wide", "narrow"), None),
            P(("wide", "narrow"), None),
            P(("wide", "narrow"), None),
            P(),
            P(),
            P(),
            P(),
        ),
        check_vma=False,
    )
```

profile of v0, /device:TPU:0, one launch (start us, length us, event | category | flops | bytes accessed | tf_op | source)
XLA Modules:
  0.0 963.6 jit_solution(3000318389720790025)
XLA Ops:
  25.4 47.6 %all-gather.5.cloned.1.call-done = bf16[768,1920]{1,0:T(8,128)(2,1)} async-done(((bf16[24,1920]{1,0:T(8,128)(2,1)}), bf16[768,1920]{1,0:T(8,128)(2,1)}) %all-gather.5.cloned.1.call-update) | async-done | bytes 2949136 | tf_op jit(solution)/shard_map/all_gather | solution.py:44
  73.0 5.6 fusion.88
  83.1 3.3 fusion.63
  92.8 77.1 %while.30 = (s32[]{:T(128)}, bf16[2,512,12,64]{1,3,2,0:T(8,128)(2,1)}, f32[2,12,512]{2,1,0:T(8,128)S(1)}, s32[2]{0:T(128)S(1)}, s32[1]{0:T(128)}, /*index=5*/bf1...) while((s32[]{:T(128)}, ...), condition=%wide.region_5.6_spmd, body=%wide.region_2.5_spmd.sunk | while | flops 1687154176 | bytes 190282096 | solution.py:171
  96.6 10.7 %fusion.136 = (f32[12,512]{1,0:T(8,128)S(1)}, f32[12,512,1024]{2,1,0:T(8,128)}) fusion(pred[512,1024]{1,0:T(8,128)(4,1)S(1)} %fusion.135, bf16[1,1024,12,64]{1,3,2,0:T(8,128)(2,1)S(1)} %get-tuple-element.609, bf16[1,1024,12,64]{1,3,2,0:T(8,128)(2,1)S(1)} %get-tuple-element.608, s32[]{:T(128)S(6)} %select_n.105), kind=kOutput, calls=%fused_computation.3.clone.1 | convolution fusion | flops 824174592 | bytes 28073988 | tf_op jit(solution)/shard_map/while/body/eval_jaxpr/qhe,khe->hqk/dot_general | solution.py:144
  107.3 12.4 %fusion.137 = f32[12,512]{1,0:T(8,128)S(1)} fusion(f32[12,512,1024]{2,1,0:T(8,128)} %get-tuple-element.562, f32[12,512]{1,0:T(8,128)S(1)} %get-tuple-element.563, pred[512,1024]{1,0:T(8,128)(4,1)S(1)} %fusion.135), kind=kLoop, calls=%fused_computation.4.clone.1 | loop fusion | flops 25159680 | bytes 25739264 | tf_op jit(solution)/shard_map/while/body/eval_jaxpr/reduce_sum | solution.py:164
  119.8 3.1 copy-done
  122.9 8.5 bitcast_dynamic-update-slice_fusion.10
  135.1 10.8 %fusion.136 = (f32[12,512]{1,0:T(8,128)S(1)}, f32[12,512,1024]{2,1,0:T(8,128)}) fusion(pred[512,1024]{1,0:T(8,128)(4,1)S(1)} %fusion.135, bf16[1,1024,12,64]{1,3,2,0:T(8,128)(2,1)S(1)} %get-tuple-element.609, bf16[1,1024,12,64]{1,3,2,0:T(8,128)(2,1)S(1)} %get-tuple-element.608, s32[]{:T(128)S(6)} %select_n.105), kind=kOutput, calls=%fused_computation.3.clone.1 | convolution fusion | flops 824174592 | bytes 28073988 | tf_op jit(solution)/shard_map/while/body/eval_jaxpr/qhe,khe->hqk/dot_general | solution.py:144
  145.8 12.3 %fusion.137 = f32[12,512]{1,0:T(8,128)S(1)} fusion(f32[12,512,1024]{2,1,0:T(8,128)} %get-tuple-element.562, f32[12,512]{1,0:T(8,128)S(1)} %get-tuple-element.563, pred[512,1024]{1,0:T(8,128)(4,1)S(1)} %fusion.135), kind=kLoop, calls=%fused_computation.4.clone.1 | loop fusion | flops 25159680 | bytes 25739264 | tf_op jit(solution)/shard_map/while/body/eval_jaxpr/reduce_sum | solution.py:164
  158.1 3.2 copy-done
  161.3 8.5 bitcast_dynamic-update-slice_fusion.10
  169.9 3.0 copy.84
  174.5 4.5 fusion.100
  181.1 14.3 %all-gather.9.cloned.1.call-done = bf16[768,3072]{1,0:T(8,128)(2,1)} async-done(((bf16[24,3072]{1,0:T(8,128)(2,1)}), bf16[768,3072]{1,0:T(8,128)(2,1)}) %all-gather.9.cloned.1.call-update) | async-done | bytes 4718608 | tf_op jit(solution)/shard_map/all_gather | solution.py:46
  195.4 11.3 %fusion.91 = f32[1024,3072]{1,0:T(8,128)} fusion(bf16[768,3072]{1,0:T(8,128)(2,1)} %all-gather.9.cloned.1.call-done, f32[1024,768]{0,1:T(8,128)} %copy-done.6, f32[768]{0:T(1024)S(1)} %copy-done.38, f32[768]{0:T(1024)S(1)} %copy-done.34, f32[1024]{0:T(1024)S(1)} %fusion.84, f32[1024]{0:T(1024)S(1)} %broadcast_multiply_fusion), kind=kOutput, calls=%fused_computation.167 | convolution fusion | flops 4835770368 | bytes 20461568 | tf_op jit(solution)/shard_map/dot_general | solution.py:177
  206.7 54.5 %all-gather.11.cloned.1.call-done = bf16[3072,768]{1,0:T(8,128)(2,1)} async-done(((bf16[96,768]{1,0:T(8,128)(2,1)}), bf16[3072,768]{1,0:T(8,128)(2,1)}) %all-gather.11.cloned.1.call-update) | async-done | bytes 4718608 | tf_op jit(solution)/shard_map/all_gather | solution.py:47
  261.2 17.7 %convert_reduce_fusion = (f32[3072]{0:T(1024)}, bf16[1024,3072]{1,0:T(8,128)(2,1)S(1)}) fusion(f32[1024,3072]{1,0:T(8,128)} %fusion.91, f32[3072]{0:T(1024)S(1)} %copy-done.62, bf16[3072,768]{1,0:T(8,128)(2,1)} %all-gather.11.cloned.1.call-done, bf16[1,1024,768]{1,2,0:T(8,128)(2,1)} %copy.86, f32[1024]{0:T(1024)S(1)} %copy-done.51), kind=kOutput, calls=%fused_computation.63 | convolution fusion | flops 4906546176 | bytes 25194496 | tf_op jit(solution)/shard_map/nd,fd->nf/dot_general | solution.py:188
  279.0 7.3 fusion.102
  286.2 3.5 copy.87
  289.8 4.5 multiply_reduce_fusion.1
  301.4 4.3 convolution_convert_fusion
  307.0 175.8 %while.31 = (s32[]{:T(128)}, bf16[2,512,12,64]{1,3,2,0:T(8,128)(2,1)}, f32[2,1024,12,64]{1,3,2,0:T(8,128)}, f32[2,1024,12,64]{1,3,2,0:T(8,128)}, s32[2]{0:T(128)...) while((s32[]{:T(128)}, ...), condition=%wide.region_12.13_spmd, body=%wide.region_10.12_spmd.sunk | while | flops 4123127296 | bytes 225630672 | solution.py:239
  312.2 11.7 %fusion.146 = f32[12,512,1024]{2,1,0:T(8,128)} fusion(bf16[1,1024,12,64]{1,3,2,0:T(8,128)(2,1)S(1)} %get-tuple-element.655, bf16[1,1024,12,64]{1,3,2,0:T(8,128)(2,1)} %copy-done.1, s32[]{:T(128)S(6)} %select_n.110), kind=kOutput, calls=%fused_computation.35.clone.1 | convolution fusion | flops 805306368 | bytes 27525124 | tf_op jit(solution)/shard_map/while/body/eval_jaxpr/qhe,khe->hqk/dot_general | solution.py:144
  324.0 13.3 %bitcast_dynamic-update-slice_fusion.14 = f32[2,1024,12,64]{1,3,2,0:T(8,128)} fusion(f32[2,1024,12,64]{1,3,2,0:T(8,128)} %get-tuple-element.635, s32[]{:T(128)S(6)} %copy.116, f32[12,512,1024]{2,1,0:T(8,128)} %fusion.146, f32[12,512]{1,0:T(8,128)S(1)} %dynamic-slice_bitcast_fusion.2, pred[512,1024]{1,0:T(8,128)(4,1)S(1)} %fusion.147, ...), kind=kOutput, calls=%fused_computation.26.clone.1 | convolution fusion | flops 830472192 | bytes 29655048 | tf_op jit(solution)/shard_map/while/body/eval_jaxpr/hqk,qhe->khe/dot_general | solution.py:234
  337.3 18.2 %multiply_reduce_fusion.10 = (f32[12,512]{1,0:T(8,128)S(1)}, f32[12,512,1024]{2,1,0:T(8,128)}) fusion(f32[12,512,1024]{2,1,0:T(8,128)} %fusion.146, f32[12,512]{1,0:T(8,128)S(1)} %dynamic-slice_bitcast_fusion.2, pred[512,1024]{1,0:T(8,128)(4,1)S(1)} %fusion.147, bf16[1,1024,12,64]{1,3,2,0:T(8,128)(2,1)} %get-tuple-element.658, ...), kind=kOutput, calls=%fused_computation.21.clone.1 | convolution fusion | flops 836757504 | bytes 53264388 | tf_op jit(solution)/shard_map/while/body/eval_jaxpr/qhe,khe->hqk/dot_general | solution.py:221
  355.5 22.0 %multiply_convert_fusion.6 = bf16[12,512,1024]{2,1,0:T(8,128)(2,1)} fusion(f32[12,512,1024]{2,1,0:T(8,128)} %get-tuple-element.575, f32[12,512,1024]{2,1,0:T(8,128)} %fusion.146, f32[12,512]{1,0:T(8,128)S(1)} %get-tuple-element.576, f32[12,512]{1,0:T(8,128)S(1)} %dynamic-slice_bitcast_fusion.2, pred[512,1024]{1,0:T(8,128)(4,1)S(1)} %fusion.147), kind=kLoop, calls=%fused_computation.20.clone.1 | loop fusion | flops 37748736 | bytes 63488000 | tf_op jit(solution)/shard_map/while/body/eval_jaxpr/convert_element_type | solution.py:225
  377.5 9.6 bitcast_dynamic-update-slice_fusion.12
  387.1 8.5 bitcast_dynamic-update-slice_fusion.13
  400.6 11.5 %fusion.146 = f32[12,512,1024]{2,1,0:T(8,128)} fusion(bf16[1,1024,12,64]{1,3,2,0:T(8,128)(2,1)S(1)} %get-tuple-element.655, bf16[1,1024,12,64]{1,3,2,0:T(8,128)(2,1)} %copy-done.1, s32[]{:T(128)S(6)} %select_n.110), kind=kOutput, calls=%fused_computation.35.clone.1 | convolution fusion | flops 805306368 | bytes 27525124 | tf_op jit(solution)/shard_map/while/body/eval_jaxpr/qhe,khe->hqk/dot_general | solution.py:144
  412.1 13.0 %bitcast_dynamic-update-slice_fusion.14 = f32[2,1024,12,64]{1,3,2,0:T(8,128)} fusion(f32[2,1024,12,64]{1,3,2,0:T(8,128)} %get-tuple-element.635, s32[]{:T(128)S(6)} %copy.116, f32[12,512,1024]{2,1,0:T(8,128)} %fusion.146, f32[12,512]{1,0:T(8,128)S(1)} %dynamic-slice_bitcast_fusion.2, pred[512,1024]{1,0:T(8,128)(4,1)S(1)} %fusion.147, ...), kind=kOutput, calls=%fused_computation.26.clone.1 | convolution fusion | flops 830472192 | bytes 29655048 | tf_op jit(solution)/shard_map/while/body/eval_jaxpr/hqk,qhe->khe/dot_general | solution.py:234
  425.1 18.2 %multiply_reduce_fusion.10 = (f32[12,512]{1,0:T(8,128)S(1)}, f32[12,512,1024]{2,1,0:T(8,128)}) fusion(f32[12,512,1024]{2,1,0:T(8,128)} %fusion.146, f32[12,512]{1,0:T(8,128)S(1)} %dynamic-slice_bitcast_fusion.2, pred[512,1024]{1,0:T(8,128)(4,1)S(1)} %fusion.147, bf16[1,1024,12,64]{1,3,2,0:T(8,128)(2,1)} %get-tuple-element.658, ...), kind=kOutput, calls=%fused_computation.21.clone.1 | convolution fusion | flops 836757504 | bytes 53264388 | tf_op jit(solution)/shard_map/while/body/eval_jaxpr/qhe,khe->hqk/dot_general | solution.py:221
  443.3 21.2 %multiply_convert_fusion.6 = bf16[12,512,1024]{2,1,0:T(8,128)(2,1)} fusion(f32[12,512,1024]{2,1,0:T(8,128)} %get-tuple-element.575, f32[12,512,1024]{2,1,0:T(8,128)} %fusion.146, f32[12,512]{1,0:T(8,128)S(1)} %get-tuple-element.576, f32[12,512]{1,0:T(8,128)S(1)} %dynamic-slice_bitcast_fusion.2, pred[512,1024]{1,0:T(8,128)(4,1)S(1)} %fusion.147), kind=kLoop, calls=%fused_computation.20.clone.1 | loop fusion | flops 37748736 | bytes 63488000 | tf_op jit(solution)/shard_map/while/body/eval_jaxpr/convert_element_type | solution.py:225
  464.5 9.5 bitcast_dynamic-update-slice_fusion.12
  474.0 8.6 bitcast_dynamic-update-slice_fusion.13
  482.8 3.0 copy.88
  487.5 3.8 reduce_sum.262
  491.3 5.7 reduce_sum.261
  498.1 8.0 fusion.68
  506.9 10.6 %fusion.90 = f32[768,3072]{1,0:T(8,128)} fusion(bf16[1024,3072]{1,0:T(8,128)(2,1)} %copy-done.70, f32[1024,768]{0,1:T(8,128)} %copy-done.6, f32[768]{0:T(1024)S(1)} %copy-done.39, f32[768]{0:T(1024)S(1)} %copy-done.35, f32[1024]{0:T(1024)S(1)} %copy-done.37, f32[1024]{0:T(1024)S(1)} %copy-done.33), kind=kOutput, calls=%fused_computation.166 | convolution fusion | flops 4835770368 | bytes 18888704 | tf_op jit(solution)/shard_map/nd,nf->df/dot_general | solution.py:193
  518.9 14.5 %fusion.73 = f32[3072,768]{1,0:T(8,128)} fusion(bf16[1,1024,768]{1,2,0:T(8,128)(2,1)S(1)} %copy-done.14, f32[1024]{0:T(1024)S(1)} %copy-done.52, f32[1024,3072]{1,0:T(8,128)} %fusion.91, f32[3072]{0:T(1024)S(1)} %copy-done.63), kind=kOutput, calls=%fused_computation.110 | convolution fusion | flops 4865654784 | bytes 23609344 | tf_op jit(solution)/shard_map/nf,nd->fd/dot_general | solution.py:184
  535.8 12.6 %fusion.72 = bf16[1,1024,768]{1,2,0:T(8,128)(2,1)} fusion(f32[1024,768]{0,1:T(8,128)} %copy-done.6, f32[768]{0:T(1024)S(1)} %copy-done.65, bf16[3072,768]{1,0:T(8,128)(2,1)} %all-gather.11.cloned.1.call-done, f32[1024]{0:T(1024)S(1)} %copy-done.52, f32[1024,3072]{1,0:T(8,128)} %fusion.91, f32[3072]{0:T(1024)S(1)} %copy-done.63), kind=kOutput, calls=%fused_computation.109 | convolution fusion | flops 4866441216 | bytes 22039552 | tf_op jit(solution)/shard_map/dot_general | solution.py:179
  554.0 9.0 fusion.101
  563.0 3.5 copy.89
  575.2 42.8 %reduce-scatter.13.cloned.1.call-done = f32[24,1920]{1,0:T(8,128)} async-done(((f32[768,1920]{1,0:T(8,128)}), f32[24,1920]{1,0:T(8,128)}) %reduce-scatter.13.cloned.1.call-update) | async-done | bytes 184336
  621.0 138.8 %reduce-scatter.9.cloned.1.call-done = f32[24,3072]{1,0:T(8,128)} async-done(((f32[768,3072]{1,0:T(8,128)}), f32[24,3072]{1,0:T(8,128)}) %reduce-scatter.9.cloned.1.call-update) | async-done | bytes 294928 | tf_op jit(solution)/shard_map/reduce_scatter | solution.py:55
  762.2 137.9 %reduce-scatter.11.cloned.1.call-done = f32[96,768]{1,0:T(8,128)} async-done(((f32[3072,768]{1,0:T(8,128)}), f32[96,768]{1,0:T(8,128)}) %reduce-scatter.11.cloned.1.call-update) | async-done | bytes 294928 | tf_op jit(solution)/shard_map/reduce_scatter | solution.py:56
  904.1 40.7 %all-reduce.1 = (f32[]{:T(128)}, f32[8832]{0:T(1024)S(1)}) all-reduce(f32[]{:T(128)S(6)} %add.344, f32[8832]{0:T(1024)S(1)} %constant_dynamic-update-slice_fusion), channel_id=1, replica_groups=mesh['wide'=8,'narrow'=4] {'wide','narrow'}, use_global_device_ids=true, to_apply=%region_25.26 | all-reduce | flops 8833 | bytes 70664 | tf_op jit(solution)/shard_map/psum | solution.py:283
  (259 shorter events, 84.2 us)
Async XLA Ops:
  7.2 13.8 %copy-start.21 = (bf16[1,1024,768]{2,1,0:T(8,128)(2,1)S(1)}, bf16[1,1024,768]{2,1,0:T(8,128)(2,1)}, u32[]{:S(2)}) copy-start(bf16[1,1024,768]{2,1,0:T(8,128)(2,1)} %param.28) | copy-start | bytes 4718596
  7.2 65.8 %all-gather.5.cloned.1.call-start = ((), (), s32[]{:S(2)}) async-start(), calls=%async_computation.4 | async-start | bytes 3041280 | tf_op jit(solution)/shard_map/all_gather | solution.py:44
  9.0 165.5 %all-gather.7.cloned.1.call-start = ((), (), s32[]{:S(2)}) async-start(), calls=%async_computation.5 | async-start | bytes 1216512 | tf_op jit(solution)/shard_map/all_gather | solution.py:45
  10.5 184.9 %all-gather.9.cloned.1.call-start = ((), (), s32[]{:S(2)}) async-start(), calls=%async_computation.6 | async-start | bytes 4866048 | tf_op jit(solution)/shard_map/all_gather | solution.py:46
  12.3 249.0 %all-gather.11.cloned.1.call-start = ((), (), s32[]{:S(2)}) async-start(), calls=%async_computation.7 | async-start | bytes 4866048 | tf_op jit(solution)/shard_map/all_gather | solution.py:47
  14.0 559.6 %reduce-scatter.7.cloned.1.call-start = ((), (), s32[]{:S(2)}) async-start(), calls=%async_computation.8 | async-start | bytes 2433024 | tf_op jit(solution)/shard_map/reduce_scatter | solution.py:54
  17.4 55.6 %copy-start.49 = (f32[768]{0:T(1024)}, f32[768]{0:T(1024)S(1)}, u32[]{:S(2)}) copy-start(f32[768]{0:T(1024)S(1)} %get-tuple-element.443) | copy-start | bytes 9220
  17.4 55.6 %copy-start.66 = (f32[768]{0:T(1024)}, f32[768]{0:T(1024)S(1)}, u32[]{:S(2)}) copy-start(f32[768]{0:T(1024)S(1)} %get-tuple-element.442) | copy-start | bytes 9220
  21.8 51.2 %copy-start.4 = (bf16[1,1024,768]{1,2,0:T(8,128)(2,1)}, bf16[1,1024,768]{1,2,0:T(8,128)(2,1)S(1)}, u32[]{:S(2)}) copy-start(bf16[1,1024,768]{1,2,0:T(8,128)(2,1)S(1)} %copy.79) | copy-start | bytes 4718596
  22.1 56.5 %copy-start.47 = (f32[1024]{0:T(1024)}, f32[1024]{0:T(1024)S(1)}, u32[]{:S(2)}) copy-start(f32[1024]{0:T(1024)S(1)} %broadcast_multiply_fusion.1) | copy-start | bytes 12292
  22.5 56.1 %copy-start.57 = (f32[1024]{0:T(1024)}, f32[1024]{0:T(1024)S(1)}, u32[]{:S(2)}) copy-start(f32[1024]{0:T(1024)S(1)} %fusion.61) | copy-start | bytes 12292
  23.8 54.9 %copy-start.53 = (f32[1024]{0:T(1024)}, f32[1024]{0:T(1024)S(1)}, u32[]{:S(2)}) copy-start(f32[1024]{0:T(1024)S(1)} %fusion.83) | copy-start | bytes 12292
  96.6 23.1 %copy-start.3 = (bf16[1,1024,12,64]{1,3,2,0:T(8,128)(2,1)S(1)}, bf16[1,1024,12,64]{1,3,2,0:T(8,128)(2,1)}, u32[]{:S(2)}) copy-start(bf16[1,1024,12,64]{1,3,2,0:T(8,128)(2,1)} %get-tuple-element.610) | copy-start | bytes 4718596 | tf_op jit(solution)/shard_map/while
  107.3 15.6 %copy-start = (f32[12,512,1024]{2,1,0:T(8,128)S(1)}, f32[12,512,1024]{2,1,0:T(8,128)}, u32[]{:S(2)}) copy-start(f32[12,512,1024]{2,1,0:T(8,128)} %get-tuple-element.562) | copy-start | bytes 75497472 | tf_op jit(solution)/shard_map/while
  135.0 23.1 %copy-start.3 = (bf16[1,1024,12,64]{1,3,2,0:T(8,128)(2,1)S(1)}, bf16[1,1024,12,64]{1,3,2,0:T(8,128)(2,1)}, u32[]{:S(2)}) copy-start(bf16[1,1024,12,64]{1,3,2,0:T(8,128)(2,1)} %get-tuple-element.610) | copy-start | bytes 4718596 | tf_op jit(solution)/shard_map/while
  145.8 15.5 %copy-start = (f32[12,512,1024]{2,1,0:T(8,128)S(1)}, f32[12,512,1024]{2,1,0:T(8,128)}, u32[]{:S(2)}) copy-start(f32[12,512,1024]{2,1,0:T(8,128)} %get-tuple-element.562) | copy-start | bytes 75497472 | tf_op jit(solution)/shard_map/while
  179.0 16.4 %copy-start.34 = (f32[768]{0:T(1024)S(1)}, f32[768]{0:T(1024)}, u32[]{:S(2)}) copy-start(f32[768]{0:T(1024)} %get-tuple-element.438) | copy-start | bytes 9220
  179.1 16.3 %copy-start.38 = (f32[768]{0:T(1024)S(1)}, f32[768]{0:T(1024)}, u32[]{:S(2)}) copy-start(f32[768]{0:T(1024)} %get-tuple-element.439) | copy-start | bytes 9220
  179.1 115.2 %copy-start.32 = (f32[1024]{0:T(1024)}, f32[1024]{0:T(1024)S(1)}, u32[]{:S(2)}) copy-start(f32[1024]{0:T(1024)S(1)} %broadcast_multiply_fusion) | copy-start | bytes 12292
  181.1 113.2 %copy-start.36 = (f32[1024]{0:T(1024)}, f32[1024]{0:T(1024)S(1)}, u32[]{:S(2)}) copy-start(f32[1024]{0:T(1024)S(1)} %fusion.84) | copy-start | bytes 12292
  195.4 65.8 %copy-start.51 = (f32[1024]{0:T(1024)S(1)}, f32[1024]{0:T(1024)}, u32[]{:S(2)}) copy-start(f32[1024]{0:T(1024)} %fusion.82) | copy-start | bytes 12292
  195.4 65.8 %copy-start.62 = (f32[3072]{0:T(1024)S(1)}, f32[3072]{0:T(1024)}, u32[]{:S(2)}) copy-start(f32[3072]{0:T(1024)} %slice.54) | copy-start | bytes 36868
  261.2 17.7 %copy-start.20 = (bf16[768,3072]{1,0:T(8,128)(2,1)S(1)}, bf16[768,3072]{1,0:T(8,128)(2,1)}, u32[]{:S(2)}) copy-start(bf16[768,3072]{1,0:T(8,128)(2,1)} %all-gather.9.cloned.1.call-done) | copy-start | bytes 14155780
  279.0 7.3 copy-start.70
  301.3 316.7 %reduce-scatter.13.cloned.1.call-start = ((), (), s32[]{:S(2)}) async-start(), calls=%async_computation.11 | async-start | bytes 6082560
  312.2 11.7 %copy-start.16 = (bf16[1,1024,12,64]{1,3,2,0:T(8,128)(2,1)S(1)}, bf16[1,1024,12,64]{1,3,2,0:T(8,128)(2,1)}, u32[]{:S(2)}) copy-start(bf16[1,1024,12,64]{1,3,2,0:T(8,128)(2,1)} %get-tuple-element.657) | copy-start | bytes 4718596 | tf_op jit(solution)/shard_map/while
  377.5 9.6 copy-start.2
  400.6 11.5 %copy-start.16 = (bf16[1,1024,12,64]{1,3,2,0:T(8,128)(2,1)S(1)}, bf16[1,1024,12,64]{1,3,2,0:T(8,128)(2,1)}, u32[]{:S(2)}) copy-start(bf16[1,1024,12,64]{1,3,2,0:T(8,128)(2,1)} %get-tuple-element.657) | copy-start | bytes 4718596 | tf_op jit(solution)/shard_map/while
  464.5 9.5 copy-start.2
  491.2 6.9 copy-start.5
  491.3 6.9 copy-start.48
  491.3 6.9 copy-start.50
  491.3 6.9 copy-start.54
  506.2 253.7 %reduce-scatter.9.cloned.1.call-start = ((), (), s32[]{:S(2)}) async-start(), calls=%async_computation.9 | async-start | bytes 9732096 | tf_op jit(solution)/shard_map/reduce_scatter | solution.py:55
  517.5 382.6 %reduce-scatter.11.cloned.1.call-start = ((), (), s32[]{:S(2)}) async-start(), calls=%async_computation.10 | async-start | bytes 9732096 | tf_op jit(solution)/shard_map/reduce_scatter | solution.py:56
  573.5 373.2 %copy-start.46 = (f32[8832]{0:T(1024)S(1)}, f32[8832]{0:T(1024)}, u32[]{:S(2)}) copy-start(f32[8832]{0:T(1024)} %param.48) | copy-start | bytes 105988
  573.5 374.7 %copy-start.40 = (f32[24,768]{1,0:T(8,128)S(1)}, f32[24,768]{1,0:T(8,128)}, u32[]{:S(2)}) copy-start(f32[24,768]{1,0:T(8,128)} %param.33) | copy-start | bytes 221188
  573.5 376.4 %copy-start.30 = (f32[24,1920]{1,0:T(8,128)S(1)}, f32[24,1920]{1,0:T(8,128)}, u32[]{:S(2)}) copy-start(f32[24,1920]{1,0:T(8,128)} %param.32) | copy-start | bytes 552964
  573.6 376.4 %copy-start.45 = (f32[24,1920]{1,0:T(8,128)S(1)}, f32[24,1920]{1,0:T(8,128)}, u32[]{:S(2)}) copy-start(f32[24,1920]{1,0:T(8,128)} %param.44) | copy-start | bytes 552964
  573.6 374.6 %copy-start.41 = (f32[24,768]{1,0:T(8,128)S(1)}, f32[24,768]{1,0:T(8,128)}, u32[]{:S(2)}) copy-start(f32[24,768]{1,0:T(8,128)} %reduce-scatter.7.cloned.1.call-done) | copy-start | bytes 221188
  618.0 331.9 %copy-start.31 = (f32[24,1920]{1,0:T(8,128)S(1)}, f32[24,1920]{1,0:T(8,128)}, u32[]{:S(2)}) copy-start(f32[24,1920]{1,0:T(8,128)} %reduce-scatter.13.cloned.1.call-done) | copy-start | bytes 552964
  761.5 190.4 %copy-start.25 = (f32[96,768]{1,0:T(8,128)S(1)}, f32[96,768]{1,0:T(8,128)}, u32[]{:S(2)}) copy-start(f32[96,768]{1,0:T(8,128)} %param.35) | copy-start | bytes 884740
  900.1 51.8 %copy-start.28 = (f32[96,768]{1,0:T(8,128)S(1)}, f32[96,768]{1,0:T(8,128)}, u32[]{:S(2)}) copy-start(f32[96,768]{1,0:T(8,128)} %reduce-scatter.11.cloned.1.call-done) | copy-start | bytes 884740
  904.0 50.2 %copy-start.26 = (f32[24,3072]{1,0:T(8,128)S(1)}, f32[24,3072]{1,0:T(8,128)}, u32[]{:S(2)}) copy-start(f32[24,3072]{1,0:T(8,128)} %param.34) | copy-start | bytes 884740
  904.0 50.2 %copy-start.27 = (f32[24,3072]{1,0:T(8,128)S(1)}, f32[24,3072]{1,0:T(8,128)}, u32[]{:S(2)}) copy-start(f32[24,3072]{1,0:T(8,128)} %reduce-scatter.9.cloned.1.call-done) | copy-start | bytes 884740
  904.0 50.2 %copy-start.42 = (f32[24,3072]{1,0:T(8,128)S(1)}, f32[24,3072]{1,0:T(8,128)}, u32[]{:S(2)}) copy-start(f32[24,3072]{1,0:T(8,128)} %param.46) | copy-start | bytes 884740
  904.0 50.2 %copy-start.43 = (f32[24,3072]{1,0:T(8,128)S(1)}, f32[24,3072]{1,0:T(8,128)}, u32[]{:S(2)}) copy-start(f32[24,3072]{1,0:T(8,128)} %param.38) | copy-start | bytes 884740
  904.0 50.2 %copy-start.44 = (f32[24,3072]{1,0:T(8,128)S(1)}, f32[24,3072]{1,0:T(8,128)}, u32[]{:S(2)}) copy-start(f32[24,3072]{1,0:T(8,128)} %param.42) | copy-start | bytes 884740
  (36 other events, 87.6 us)
Sparse Core Ops, SparseCore 0:
  11.5 61.4 all-gather.4
  76.5 52.8 all-gather.6
  132.8 62.5 all-gather.8
  198.7 62.4 all-gather.10
  301.4 97.8 reduce-scatter.6
  506.3 111.7 reduce-scatter.12
  624.9 134.8 reduce-scatter.8
  765.7 134.3 reduce-scatter.10
where the time goes:
time: 971 us; the launch traced here: 964 us
  waiting for transfers between devices  436 us (45%)
  matrix products  269 us (28%)
  other arithmetic  125 us (13%)
  local copies, waits for them, and re-layouts  60.9 us (6%)
  blocking collectives  40.7 us (4%)
  between operations  20.9 us (2%)
  loops' own time  11.2 us (1%)
    reduce_scatter x1, waiting for transfers between devices, sum_gradients(): lax.psum_scatter(partials[2], ('wide', 'narrow'), scatter_dimension=0, ti...  139 us
    reduce_scatter x1, waiting for transfers between devices, sum_gradients(): lax.psum_scatter(partials[3], ('wide', 'narrow'), scatter_dimension=0, ti...  138 us
    all_gather x1, waiting for transfers between devices, gather_copies(): lax.all_gather(lowered[3], ('wide', 'narrow'), axis=0, tiled=True)  54.5 us
    all_gather x1, waiting for transfers between devices, gather_copies(): lax.all_gather(lowered[0], ('wide', 'narrow'), axis=0, tiled=True)  47.6 us
    dot_general x4, matrix products, masked_scores(): jnp.einsum('qhe,khe->hqk', query_block, key_slot, preferred_element_type=...  44.6 us
    convert_element_type x2, other arithmetic, backward_block(): grad_scores = (probs * (grad_probs - inner)).astype(jnp.bfloat16)  43.3 us
    unnamed x9, waiting for transfers between devices  43 us
    psum x1, blocking collectives, body(): lax.psum((vector_partial, local_squares), ('wide', 'narrow'))  40.7 us
  transfers between devices with their start and end apart: 8, of which 6 were waited for; matrix products, arithmetic and copies ran while one was open for 40% of the time, Pallas kernels for 0%

commit v1 on v0

--- a/solution.py
+++ b/solution.py
@@ -1,8 +1,359 @@
 import jax
 import jax.numpy as jnp
 from jax import lax
+from jax.experimental import pallas as pl
+from jax.experimental.pallas import tpu as pltpu
 from jax.sharding import PartitionSpec as P
 
+import functools
+bf=jnp.bfloat16; f32=jnp.float32
+MESH=pl.DeviceIdType.MESH
+D = 768
+FF = 3072
+WIN=1920; WPAD=2048
+
+class Place:
+    def __init__(s):
+        s.w=lax.axis_index("wide"); s.n=lax.axis_index("narrow")
+        s.z=s.w//2; s.y=s.w%2; s.x=s.n//2; s.c=s.n%2
+        s.sib=(s.w,s.n+1-2*s.c); s.xn=(s.w,(s.n+2)%4); s.yn=(s.w+1-2*s.y,s.n)
+        s.chip=s.z*4+s.y*2+s.x
+    def zdev(s,zt): return (zt*2+s.y,s.n)
+    def p(s,zt,dy,dx):
+        yy=s.y if not dy else 1-s.y
+        xx=s.x if not dx else 1-s.x
+        return zt*4+yy*2+xx
+
+def rcopy(src,dst,ss,rs,dev):
+    return pltpu.make_async_remote_copy(src_ref=src,dst_ref=dst,send_sem=ss,recv_sem=rs,device_id=dev,device_id_type=MESH)
+
+def entry_barrier(P):
+    bar=pltpu.get_barrier_semaphore()
+    devs=[P.sib,P.xn,P.yn]
+    for d in devs: pl.semaphore_signal(bar,inc=1,device_id=d,device_id_type=MESH)
+    for k in (1,2,3):
+        pl.semaphore_signal(bar,inc=1,device_id=P.zdev((P.z+k)%4),device_id_type=MESH)
+    pl.semaphore_wait(bar,6)
+
+NSEM=16
+class Gather:
+    def __init__(g,P,W,col0,hc,rb,ss,rs):
+        g.P,g.W,g.col0,g.hc,g.rb,g.ss,g.rs=P,W,col0,hc,rb,ss,rs
+    def view(g,p,h=None):
+        h=g.P.c if h is None else h
+        return g.W.at[pl.ds(pl.multiple_of(p*g.rb,g.rb),g.rb),pl.ds(pl.multiple_of(g.col0+h*g.hc,128),g.hc)]
+    def half(g,h):
+        return g.W.at[:,pl.ds(pl.multiple_of(g.col0+h*g.hc,128),g.hc)]
+    def put(g,p,i,dev):
+        v=g.view(p); rcopy(v,v,g.ss.at[i],g.rs.at[i],dev).start()
+    def got(g,p,i):
+        v=g.view(p); rcopy(v,v,g.ss.at[i],g.rs.at[i],g.P.sib).wait_recv()
+    def zk(g,k): return (g.P.z+4-k)%4
+    def spread(g,p,k):
+        g.put(p,3+k,g.P.xn); g.put(p,9+k,g.P.yn); g.put(p,15,g.P.sib)
+    def start(g):
+        P=g.P; p=P.chip
+        for k in (1,2,3): g.put(p,k-1,P.zdev((P.z+k)%4))
+        g.spread(p,0)
+    def step_z(g):
+        for k in (1,2,3):
+            p=g.P.p(g.zk(k),0,0)
+            g.got(p,k-1); g.spread(p,k)
+    def step_xy(g):
+        P=g.P
+        for k in range(4):
+            px=P.p(g.zk(k),0,1); py=P.p(g.zk(k),1,0)
+            g.got(px,3+k)
+            if k<2: g.put(px,13+k,P.yn)
+            g.put(px,15,P.sib)
+            g.got(py,9+k)
+            if k>=2: g.put(py,5+k,P.xn)
+            g.put(py,15,P.sib)
+    def step_d(g):
+        P=g.P
+        for k in range(4):
+            pd=P.p(g.zk(k),1,1)
+            g.got(pd,13+k if k<2 else 5+k)
+            g.put(pd,15,P.sib)
+    def finish(g):
+        v=g.half(1-g.P.c)
+        rcopy(v,v,g.ss.at[15],g.rs.at[15],g.P.sib).wait_recv()
+    def drain(g):
+        v=g.view(g.P.chip)
+        for i in range(15): rcopy(v,v,g.ss.at[i],g.rs.at[i],g.P.sib).wait_send()
+        v=g.half(g.P.c)
+        rcopy(v,v,g.ss.at[15],g.rs.at[15],g.P.sib).wait_send()
+
+class GatherPlane:
+    def __init__(g,P,W,b,hc,rb,ss,rs):
+        g.P,g.W,g.b,g.hc,g.rb,g.ss,g.rs=P,W,b,hc,rb,ss,rs
+    def view(g,p,part=None):
+        r0,n=p*g.rb,g.rb
+        if part is not None: n=g.rb//2; r0=r0+part*n
+        return g.W.at[pl.ds(pl.multiple_of(r0,n),n),pl.ds(pl.multiple_of(g.P.c*g.hc,128),g.hc)]
+    def half(g,h):
+        return g.W.at[pl.ds(g.b*4*g.rb,4*g.rb),pl.ds(pl.multiple_of(h*g.hc,128),g.hc)]
+    def put(g,p,i,dev,part=None):
+        v=g.view(p,part); rcopy(v,v,g.ss.at[i],g.rs.at[i],dev).start()
+    def got(g,p,i,part=None):
+        v=g.view(p,part); rcopy(v,v,g.ss.at[i],g.rs.at[i],g.P.sib).wait_recv()
+    def start(g):
+        P=g.P
+        @pl.when(P.z==g.b)
+        def _():
+            for k in (1,2,3): g.put(P.chip,k-1,P.zdev((P.z+k)%4))
+    def step_z(g):
+        P=g.P; p=P.p(g.b,0,0)
+        @pl.when(P.z!=g.b)
+        def _():
+            k=(P.z+4-g.b)%4
+            v=g.view(p); rcopy(v,v,g.ss.at[k-1],g.rs.at[k-1],P.sib).wait_recv()
+        g.put(p,3,P.xn); g.put(p,4,P.yn); g.put(p,15,P.sib)
+    def step_xy(g):
+        P=g.P; px=P.p(g.b,0,1); py=P.p(g.b,1,0)
+        g.got(px,3); g.put(px,5,P.yn,0); g.put(px,15,P.sib)
+        g.got(py,4); g.put(py,6,P.xn,1); g.put(py,15,P.sib)
+    def step_d(g):
+        P=g.P; pd=P.p(g.b,1,1)
+        g.got(pd,5,0); g.got(pd,6,1); g.put(pd,15,P.sib)
+    def finish(g):
+        v=g.half(1-g.P.c)
+        rcopy(v,v,g.ss.at[15],g.rs.at[15],g.P.sib).wait_recv()
+    def drain(g):
+        P=g.P; v=g.view(P.chip)
+        @pl.when(P.z==g.b)
+        def _():
+            for i in range(3): rcopy(v,v,g.ss.at[i],g.rs.at[i],P.sib).wait_send()
+        for i in (3,4): rcopy(v,v,g.ss.at[i],g.rs.at[i],P.sib).wait_send()
+        v=g.view(P.chip,0)
+        for i in (5,6): rcopy(v,v,g.ss.at[i],g.rs.at[i],P.sib).wait_send()
+        v=g.half(P.c)
+        rcopy(v,v,g.ss.at[15],g.rs.at[15],P.sib).wait_send()
+
+def rows(ref,r0,n,c0,m):
+    return ref.at[pl.ds(pl.multiple_of(r0,n),n),pl.ds(pl.multiple_of(c0,128),m)]
+
+class Reduce:
+    def __init__(g,P,G,col0,hc,rb,R,X,F,ss,rs):
+        g.P,g.G,g.col0,g.hc,g.rb,g.R,g.X,g.F,g.ss,g.rs=P,G,col0,hc,rb,R,X,F,ss,rs
+    def cs(g,h): return pl.ds(pl.multiple_of(g.col0+h*g.hc,128),g.hc)
+    def view(g,p): return g.G.at[pl.ds(pl.multiple_of(p*g.rb,g.rb),g.rb),g.cs(g.P.c)]
+    def rs_(g,p): return pl.ds(pl.multiple_of(p*g.rb,g.rb),g.rb)
+    def start(g):
+        P=g.P
+        g.d0=rcopy(g.G.at[:,g.cs(1-P.c)],g.R,g.ss.at[15],g.rs.at[15],P.sib); g.d0.start()
+    def put(g,p,i,dev):
+        rcopy(g.view(p),g.X.at[i],g.ss.at[i],g.rs.at[i],dev).start()
+    def got(g,i):
+        v=g.X.at[i]; rcopy(v,v,g.ss.at[i],g.rs.at[i],g.P.sib).wait_recv()
+    def addR(g,p):
+        g.G[g.rs_(p),g.cs(g.P.c)]=(g.G[g.rs_(p),g.cs(g.P.c)].astype(f32)+g.R[g.rs_(p),:].astype(f32)).astype(bf)
+    def step_c(g):
+        P=g.P
+        g.d0.wait_recv()
+        for zt in range(4):
+            p=P.p(zt,1,1); g.addR(p)
+            g.put(p,zt,P.yn if zt<2 else P.xn)
+        for zt in range(4):
+            for dy,dx in ((0,1),(1,0),(0,0)): g.addR(P.p(zt,dy,dx))
+    def addX(g,p,i):
+        g.G[g.rs_(p),g.cs(g.P.c)]=(g.G[g.rs_(p),g.cs(g.P.c)].astype(f32)+g.X[i].astype(f32)).astype(bf)
+    def step_d(g):
+        P=g.P
+        for zt in range(4):
+            px=P.p(zt,0,1); py=P.p(zt,1,0)
+            g.got(zt)
+            if zt<2: g.addX(px,zt)
+            else: g.addX(py,zt)
+            g.put(px,4+zt,P.xn); g.put(py,8+zt,P.yn)
+    def step_xy(g):
+        P=g.P
+        for k in (1,2,3,0):
+            zt=(P.z+k)%4
+            v=g.X.at[4+zt]; rcopy(v,v,g.ss.at[4+zt],g.rs.at[4+zt],P.sib).wait_recv()
+            v=g.X.at[8+zt]; rcopy(v,v,g.ss.at[8+zt],g.rs.at[8+zt],P.sib).wait_recv()
+            p=P.p(zt,0,0)
+            s=g.G[g.rs_(p),g.cs(P.c)].astype(f32)+g.X[4+zt].astype(f32)+g.X[8+zt].astype(f32)
+            if k:
+                g.G[g.rs_(p),g.cs(P.c)]=s.astype(bf)
+                g.put(p,11+k,P.zdev(zt))
+            else: g.F[...]=s
+    def step_z(g):
+        s=g.F[...]
+        for k in (1,2,3):
+            g.got(11+k); s=s+g.X[11+k].astype(f32)
+        g.F[...]=s
+        return jnp.sum(s*s,axis=0,keepdims=True)
+    def drain(g):
+        P=g.P
+        for i in range(15):
+            rcopy(g.view(P.chip),g.X.at[i],g.ss.at[i],g.rs.at[i],P.sib).wait_send()
+        g.d0.wait_send()
+
+class ReducePlane:
+    def __init__(g,P,G,b,hc,rb,R,X,F,ss,rs):
+        g.P,g.G,g.b,g.hc,g.rb,g.R,g.X,g.F,g.ss,g.rs=P,G,b,hc,rb,R,X,F,ss,rs
+    def cs(g,h): return pl.ds(pl.multiple_of(h*g.hc,128),g.hc)
+    def rs_(g,p,part=None,local=False):
+        n=g.rb
+        r0=(p-4*g.b if local else p)*n
+        if part is not None: n=n//2; r0=r0+part*n
+        return pl.ds(pl.multiple_of(r0,n),n)
+    def start(g):
+        P=g.P
+        g.d0=rcopy(g.G.at[pl.ds(g.b*4*g.rb,4*g.rb),g.cs(1-P.c)],g.R,g.ss.at[15],g.rs.at[15],P.sib); g.d0.start()
+    def view(g,p,part=None): return g.G.at[g.rs_(p,part),g.cs(g.P.c)]
+    def xv(g,i,part=None):
+        if part is None: return g.X.at[i]
+        return g.X.at[i,pl.ds(part*(g.rb//2),g.rb//2)]
+    def cp(g,p,i,sem,dev,part=None):
+        return rcopy(g.view(p,part),g.xv(i,part),g.ss.at[sem],g.rs.at[sem],dev)
+    def addR(g,p):
+        a=g.G[g.rs_(p),g.cs(g.P.c)].astype(f32)+g.R[g.rs_(p,None,True),:].astype(f32)
+        g.G[g.rs_(p),g.cs(g.P.c)]=a.astype(bf)
+    def step_c(g):
+        P=g.P; g.d0.wait_recv()
+        pd=P.p(g.b,1,1); g.addR(pd)
+        g.cp(pd,0,0,P.yn,0).start(); g.cp(pd,0,1,P.xn,1).start()
+        for dy,dx in ((0,1),(1,0),(0,0)): g.addR(P.p(g.b,dy,dx))
+    def step_d(g):
+        P=g.P; h=g.rb//2
+        for part,(p,sem,dev,i) in enumerate(((P.p(g.b,0,1),0,P.xn,1),(P.p(g.b,1,0),1,P.yn,2))):
+            g.cp(p,0,sem,P.sib,part).wait_recv()
+            a=g.G[g.rs_(p,part),g.cs(P.c)].astype(f32)+g.X[0,part*h:part*h+h].astype(f32)
+            g.G[g.rs_(p,part),g.cs(P.c)]=a.astype(bf)
+            g.cp(p,i,1+i,dev).start()
+    def step_xy(g):
+        P=g.P; p=P.p(g.b,0,0)
+        g.cp(p,1,2,P.sib).wait_recv(); g.cp(p,2,3,P.sib).wait_recv()
+        s=g.G[g.rs_(p),g.cs(P.c)].astype(f32)+g.X[1].astype(f32)+g.X[2].astype(f32)
+        g.F[...]=s
+        @pl.when(P.z!=g.b)
+        def _():
+            g.G[g.rs_(p),g.cs(P.c)]=s.astype(bf)
+            k=(P.z+4-g.b)%4
+            rcopy(g.view(p),g.X.at[2+k],g.ss.at[4],g.rs.at[3+k],P.zdev(g.b)).start()
+    def step_z(g,FD):
+        P=g.P; p=P.p(g.b,0,0)
+        @pl.when(P.z==g.b)
+        def _():
+            s=g.F[...]
+            for k in (1,2,3):
+                v=g.X.at[2+k]; rcopy(v,v,g.ss.at[4],g.rs.at[3+k],P.sib).wait_recv()
+                s=s+g.X[2+k].astype(f32)
+            FD[...]=s
+    def drain(g):
+        P=g.P; p=P.chip
+        g.cp(p,0,0,P.sib,0).wait_send(); g.cp(p,0,1,P.sib,1).wait_send()
+        g.cp(p,1,2,P.sib).wait_send(); g.cp(p,2,3,P.sib).wait_send()
+        @pl.when(P.z!=g.b)
+        def _(): g.cp(p,1,4,P.sib).wait_send()
+        g.d0.wait_send()
+
+HBM=pl.BlockSpec(memory_space=pl.ANY)
+
+def gather_kernel(wi,wo,wu,wd,oi,oo,ou,od,Wi,Wo,Wu,Wd,Xi,Xo,Xu,Xd,ss,rs,es,er,ls,os_):
+    P=Place()
+    entry_barrier(P)
+    pre=[]
+    for i,(s,X) in enumerate(((wi,Xi),(wo,Xo),(wu,Xu),(wd,Xd))):
+        dst=X.at[P.c]
+        if i==0: dst=X.at[P.c,:,pl.ds(0,WIN)]
+        r=rcopy(s,dst,es.at[i],er.at[i],P.sib); r.start()
+        l=pltpu.make_async_copy(s,dst,ls.at[i]); l.start()
+        pre.append((r,l))
+    def pack(i,X,W,n,cols,hc):
+        r,l=pre[i]; r.wait(); l.wait()
+        for h in range(1):
+            v=jnp.concatenate([X[0,:,cols],X[1,:,cols]],axis=0).astype(bf)
+            W[pl.ds(pl.multiple_of(P.chip*n,n),n),cols]=v
+    Xi[:,:,1920:]=jnp.zeros((2,24,128),f32)
+    c=P.c
+    def cc(hc,o=0): return pl.ds(pl.multiple_of(o+c*hc,128),hc)
+    pack(0,Xi,Wi,48,cc(1024),1024)
+    items=[Gather(P,Wi,0,1024,48,ss.at[0],rs.at[0])]
+    items[0].start()
+    pack(1,Xo,Wo,48,cc(384),384)
+    items.append(Gather(P,Wo,0,384,48,ss.at[1],rs.at[1])); items[1].start()
+    for b in range(4):
+        if b==0:
+            r,l=pre[2]; r.wait(); l.wait()
+            r,l=pre[3]; r.wait(); l.wait()
+            W=Wd; cols=cc(384)
+            W[pl.ds(pl.multiple_of(P.chip*192,192),192),cols]=jnp.concatenate([Xd[0,:,cols],Xd[1,:,cols]],axis=0).astype(bf)
+        cols=cc(384,768*b)
+        Wu[pl.ds(pl.multiple_of(P.chip*48,48),48),cols]=jnp.concatenate([Xu[0,:,cols],Xu[1,:,cols]],axis=0).astype(bf)
+        g=Gather(P,Wu,768*b,384,48,ss.at[2+2*b],rs.at[2+2*b]); g.start(); items.append(g)
+        g=GatherPlane(P,Wd,b,384,192,ss.at[3+2*b],rs.at[3+2*b]); g.start(); items.append(g)
+    stages=["step_z","step_xy","step_d","finish"]
+    n=len(items)
+    for t in range(n+len(stages)-1):
+        for s in reversed(range(len(stages))):
+            i=t-s
+            if 0<=i<n: getattr(items[i],stages[s])()
+    for g in items: g.drain()
+    cps=[]
+    for i,(a,b) in enumerate(((Wi,oi),(Wo,oo),(Wu,ou),(Wd,od))):
+        cp=pltpu.make_async_copy(a,b,os_.at[i]); cp.start(); cps.append(cp)
+    for cp in cps: cp.wait()
+
+def gather_weights(wi,wo,wu,wd):
+    V=pltpu.VMEM; S=pltpu.SemaphoreType.DMA
+    sh=lambda s: jax.ShapeDtypeStruct(s,bf)
+    return pl.pallas_call(gather_kernel,out_shape=[sh((D,WPAD)),sh((D,D)),sh((D,FF)),sh((FF,D))],
+      in_specs=[HBM]*4,out_specs=[HBM]*4,
+      scratch_shapes=[V((D,WPAD),bf),V((D,D),bf),V((D,FF),bf),V((FF,D),bf),V((2,24,WPAD),f32),V((2,24,D),f32),V((2,24,FF),f32),V((2,96,D),f32),
+        S((10,16)),S((10,16)),S((4,)),S((4,)),S((4,)),S((4,))],
+      compiler_params=pltpu.CompilerParams(collective_id=1,has_side_effects=True,vmem_limit_bytes=60<<20))(wi,wo,wu,wd)
+
+def reduce_kernel(gi,go,gu,gd,oi,oo,ou,od,sq,Gi,Go,Gu,Gd,Ri,Ro,Ru,Rd,Xi,Xo,Xu,Xd,Fi,Fo,Fu,Fp,Fd,ss,rs,ls,es,er,fs):
+    P=Place()
+    entry_barrier(P)
+    cps=[]
+    for i,(a,b) in enumerate(((gi,Gi),(go,Go),(gu,Gu),(gd,Gd))):
+        cp=pltpu.make_async_copy(a,b,ls.at[i]); cp.start(); cps.append(cp)
+    for cp in cps: cp.wait()
+    items=[]
+    for b in range(4):
+        items.append(Reduce(P,Gu,768*b,384,48,Ru.at[b],Xu.at[b],Fu.at[b],ss.at[2+2*b],rs.at[2+2*b]))
+        items.append(ReducePlane(P,Gd,b,384,192,Rd.at[b],Xd.at[b],Fp.at[b],ss.at[3+2*b],rs.at[3+2*b]))
+    items.append(Reduce(P,Go,0,384,48,Ro,Xo,Fo,ss.at[1],rs.at[1]))
+    items.append(Reduce(P,Gi,0,1024,48,Ri,Xi,Fi,ss.at[0],rs.at[0]))
+    tot=[]
+    def last(g):
+        if isinstance(g,ReducePlane): g.step_z(Fd)
+        else: tot.append(jnp.sum(g.step_z(),axis=1,keepdims=True))
+    stages=["start","step_c","step_d","step_xy",None]
+    n=len(items)
+    for t in range(n+len(stages)-1):
+        for s in reversed(range(len(stages))):
+            i=t-s
+            if 0<=i<n:
+                if s==4: last(items[i])
+                else: getattr(items[i],stages[s])()
+    tot.append(jnp.sum(jnp.sum(Fd[...]*Fd[...],axis=0,keepdims=True),axis=1,keepdims=True))
+    sq[...]=jnp.broadcast_to(sum(tot),(8,128))
+    c=P.c; fin=[]
+    e=0
+    for F,O,c0,hc,n in [(Fi,oi,0,1024,24),(Fo,oo,0,384,24)]+[(Fu.at[b],ou,768*b,384,24) for b in range(4)]+[(Fd,od,0,384,96)]:
+        cols=pl.ds(pl.multiple_of(c0+c*hc,128),hc)
+        r=rcopy(F.at[pl.ds(pl.multiple_of((1-c)*n,8),n)],O.at[:,cols],es.at[e],er.at[e],P.sib); r.start()
+        l=pltpu.make_async_copy(F.at[pl.ds(pl.multiple_of(c*n,8),n)],O.at[:,cols],fs.at[e]); l.start()
+        fin+= [r,l]; e+=1
+    for f in fin: f.wait()
+    for g in items: g.drain()
+
+def reduce_grads(gi,go,gu,gd):
+    V=pltpu.VMEM; S=pltpu.SemaphoreType.DMA
+    sh=lambda s: jax.ShapeDtypeStruct(s,f32)
+    return pl.pallas_call(reduce_kernel,out_shape=[sh((24,WPAD)),sh((24,D)),sh((24,FF)),sh((96,D)),sh((8,128))],
+      in_specs=[HBM]*4,out_specs=[HBM]*4+[pl.BlockSpec(memory_space=pltpu.VMEM)],
+      scratch_shapes=[V((D,WPAD),bf),V((D,D),bf),V((D,FF),bf),V((FF,D),bf),
+        V((D,1024),bf),V((D,384),bf),V((4,D,384),bf),V((4,D,384),bf),
+        V((15,48,1024),bf),V((15,48,384),bf),V((4,15,48,384),bf),V((4,6,192,384),bf),
+        V((48,1024),f32),V((48,384),f32),V((4,48,384),f32),V((4,192,384),f32),V((192,384),f32),
+        S((10,16)),S((10,16)),S((4,)),S((7,)),S((7,)),S((7,))],
+      compiler_params=pltpu.CompilerParams(collective_id=2,has_side_effects=True,vmem_limit_bytes=60<<20))(gi,go,gu,gd)
 D = 768
 H = 12
 HD = 64
@@ -95,7 +446,12 @@
 ):
     masters = (weight_in, weight_out, weight_up, weight_down)
     lowered = tuple((master.astype(jnp.bfloat16) for master in masters))
-    copies = gather_copies(lowered)
+    custom = MESH_SIZES == (8, 4)
+    if custom:
+        gathered = gather_weights(*masters)
+        copies = (gathered[0][:, :WIN],) + tuple(gathered[1:])
+    else:
+        copies = gather_copies(lowered)
     slot_count, seq_len = (tokens.shape[0], tokens.shape[1])
     row_count = slot_count * seq_len
     span = H * HD
@@ -178,7 +534,7 @@
     active_low = jax.nn.gelu(hidden_pre, approximate=True).astype(jnp.bfloat16)
     feed = jnp.dot(active_low, copies[3], preferred_element_type=jnp.float32) + bias_down
     result = (valid * (middle + feed)).astype(jnp.bfloat16).reshape(slot_count, seq_len, D)
-    back_copies = gather_copies(lowered)
+    back_copies = copies
     grad_out = cotangent.astype(jnp.float32).reshape(row_count, D) * valid
     grad_out_low = grad_out.astype(jnp.bfloat16)
     grad_down = jnp.einsum(
@@ -263,7 +619,13 @@
     grad_tokens = (
         (grad_middle + grad_inputs_norm).astype(jnp.bfloat16).reshape(slot_count, seq_len, D)
     )
-    shards = sum_gradients((grad_weight_in, grad_weight_out, grad_up, grad_down))
+    if custom:
+        low = tuple(g.astype(jnp.bfloat16) for g in (grad_weight_in, grad_weight_out, grad_up, grad_down))
+        padded = jnp.pad(low[0], ((0, 0), (0, WPAD - WIN)))
+        *shards, squares = reduce_grads(padded, *low[1:])
+        shards[0] = shards[0][:, :WIN]
+    else:
+        shards = sum_gradients((grad_weight_in, grad_weight_out, grad_up, grad_down))
     local_squares = jnp.float32(0.0)
     for shard in shards:
         local_squares = local_squares + jnp.sum(shard * shard)
@@ -315,6 +677,8 @@
 
 
 def solution(mesh):
+    global MESH_SIZES
+    MESH_SIZES = (mesh.shape["wide"], mesh.shape["narrow"])
     return jax.shard_map(
         body,
         mesh=mesh,

time: 971 us -> 677 us (0.70)
  waiting for transfers between devices: 436 us -> 0 us
  Pallas kernels: 0 us -> 182 us
  between operations: 20.9 us -> 7.67 us
  matrix products: 269 us -> 258 us
    reduce_scatter x3 -> x0, waiting for transfers between devices: 277 us -> none  [the longest x1 139 us: sum_gradients(): lax.psum_scatter(partials[2], ('wide', 'narrow'), scatter_dimension=0, ti...]
    pallas_call x0 -> x2, Pallas kernels: none -> 182 us  [the longest x1 92 us: reduce_grads(): pl.pallas_call(reduce_kernel, out_shape=[sh((24, WPAD)), sh((24, D)), sh(...]
    all_gather x4 -> x0, waiting for transfers between devices: 116 us -> none  [the longest x1 54.5 us: gather_copies(): lax.all_gather(lowered[3], ('wide', 'narrow'), axis=0, tiled=True)]
    unnamed x9 -> x0, waiting for transfers between devices: 43 us -> none
    unnamed x148 -> x166, local copies, waits for them, and re-layouts: 27.9 us -> 20.3 us
  transfers between devices with their start and end apart: 8 -> 0, of which waited for: 6 -> 0; matrix products, arithmetic and copies ran while one was open for 40% -> 0% of each run, Pallas kernels for 0% -> 0%
where the time goes in v1:
time: 677 us; the launch traced here: 669 us
  matrix products  258 us (38%)
  Pallas kernels  182 us (27%)
  other arithmetic  116 us (17%)
  local copies, waits for them, and re-layouts  54.6 us (8%)
  blocking collectives  40.3 us (6%)
  loops' own time  11.6 us (2%)
  between operations  7.67 us (1%)
    pallas_call x1, Pallas kernels, reduce_grads(): pl.pallas_call(reduce_kernel, out_shape=[sh((24, WPAD)), sh((24, D)), sh(...  92 us
    pallas_call x1, Pallas kernels, gather_weights(): pl.pallas_call(gather_kernel, out_shape=[sh((D, WPAD)), sh((D, D)), sh((D...  89.5 us
    dot_general x4, matrix products, masked_scores(): jnp.einsum('qhe,khe->hqk', query_block, key_slot, preferred_element_type=...  44 us
    convert_element_type x2, other arithmetic, backward_block(): grad_scores = (probs * (grad_probs - inner)).astype(jnp.bfloat16)  42.5 us
    psum x1, blocking collectives, body(): lax.psum((vector_partial, local_squares), ('wide', 'narrow'))  40.3 us
    dot_general x2, matrix products, backward_block(): jnp.einsum('qhe,khe->hqk', grad_block, value_slot, preferred_element_type...  36.2 us
    dot_general x2, matrix products, backward_block(): jnp.einsum('hqk,qhe->khe', probs_low, grad_block, preferred_element_type=...  26.1 us
    reduce_sum x2, other arithmetic, forward_block(): summed = jnp.sum(exponent, axis=-1, keepdims=True)  24.6 us

profile of v1, /device:TPU:0, one launch (start us, length us, event | category | flops | bytes accessed | tf_op | source)
XLA Modules:
  0.0 669.4 jit_solution(17268604765053283024)
XLA Ops:
  9.8 2.6 copy.70
  12.4 89.5 %shard_map.415 = (bf16[768,2048]{1,0:T(8,128)(2,1)}, bf16[768,768]{1,0:T(8,128)(2,1)}, bf16[768,3072]{1,0:T(8,128)(2,1)}, bf16[3072,768]{1,0:T(8,128)(2,1)}) custom-call(f32[24,1920]{1,0:T(8,128)} %wi.1, f32[24,768]{1,0:T(8,128)} %wo.1, f32[24,3072]{1,0:T(8,128)} %wu.1, f32[96,768]{1,0:T(8,128)} %wd.1), custom_call_target="tpu_custom_call" | custom-call | tf_op jit(solution)/shard_map/pallas_call | solution.py:303
  101.9 5.5 fusion.69
  107.5 3.0 copy-done.17
  112.2 3.3 fusion.63
  121.4 76.8 %while.30 = (s32[]{:T(128)}, bf16[2,512,12,64]{1,3,2,0:T(8,128)(2,1)}, f32[2,12,512]{2,1,0:T(8,128)S(1)}, s32[2]{0:T(128)S(1)}, s32[1]{0:T(128)}, /*index=5*/bf1...) while((s32[]{:T(128)}, ...), condition=%wide.region_5.6_spmd, body=%wide.region_2.5_spmd.sunk | while | flops 1687154176 | bytes 190282096 | solution.py:527
  125.5 10.6 %fusion.132 = (f32[12,512]{1,0:T(8,128)S(1)}, f32[12,512,1024]{2,1,0:T(8,128)}) fusion(pred[512,1024]{1,0:T(8,128)(4,1)S(1)} %fusion.131, bf16[1,1024,12,64]{1,3,2,0:T(8,128)(2,1)S(1)} %get-tuple-element.601, bf16[1,1024,12,64]{1,3,2,0:T(8,128)(2,1)S(1)} %get-tuple-element.600, s32[]{:T(128)S(6)} %select_n.105), kind=kOutput, calls=%fused_computation.3.clone.1 | convolution fusion | flops 824174592 | bytes 28073988 | tf_op jit(solution)/shard_map/while/body/eval_jaxpr/qhe,khe->hqk/dot_general | solution.py:500
  136.1 12.3 %fusion.133 = f32[12,512]{1,0:T(8,128)S(1)} fusion(f32[12,512,1024]{2,1,0:T(8,128)} %get-tuple-element.554, f32[12,512]{1,0:T(8,128)S(1)} %get-tuple-element.555, pred[512,1024]{1,0:T(8,128)(4,1)S(1)} %fusion.131), kind=kLoop, calls=%fused_computation.4.clone.1 | loop fusion | flops 25159680 | bytes 25739264 | tf_op jit(solution)/shard_map/while/body/eval_jaxpr/reduce_sum | solution.py:520
  148.4 3.1 copy-done
  151.5 8.5 %bitcast_dynamic-update-slice_fusion.10 = bf16[2,512,12,64]{1,3,2,0:T(8,128)(2,1)} fusion(bf16[2,512,12,64]{1,3,2,0:T(8,128)(2,1)} %get-tuple-element.583, s32[]{:T(128)S(6)} %copy.90, bf16[1,1024,12,64]{1,3,2,0:T(8,128)(2,1)S(1)} %copy-done.3, f32[12,512,1024]{2,1,0:T(8,128)S(1)} %copy-done, f32[12,512]{1,0:T(8,128)S(1)} %fusion.133, ...), kind=kOutput, calls=%fused_computation.8.clone.1 | convolution fusion | flops 836763648 | bytes 28884996 | tf_op jit(solution)/shard_map/while/body/eval_jaxpr/hqk,khe->qhe/dot_general | solution.py:522
  163.6 10.6 %fusion.132 = (f32[12,512]{1,0:T(8,128)S(1)}, f32[12,512,1024]{2,1,0:T(8,128)}) fusion(pred[512,1024]{1,0:T(8,128)(4,1)S(1)} %fusion.131, bf16[1,1024,12,64]{1,3,2,0:T(8,128)(2,1)S(1)} %get-tuple-element.601, bf16[1,1024,12,64]{1,3,2,0:T(8,128)(2,1)S(1)} %get-tuple-element.600, s32[]{:T(128)S(6)} %select_n.105), kind=kOutput, calls=%fused_computation.3.clone.1 | convolution fusion | flops 824174592 | bytes 28073988 | tf_op jit(solution)/shard_map/while/body/eval_jaxpr/qhe,khe->hqk/dot_general | solution.py:500
  174.3 12.3 %fusion.133 = f32[12,512]{1,0:T(8,128)S(1)} fusion(f32[12,512,1024]{2,1,0:T(8,128)} %get-tuple-element.554, f32[12,512]{1,0:T(8,128)S(1)} %get-tuple-element.555, pred[512,1024]{1,0:T(8,128)(4,1)S(1)} %fusion.131), kind=kLoop, calls=%fused_computation.4.clone.1 | loop fusion | flops 25159680 | bytes 25739264 | tf_op jit(solution)/shard_map/while/body/eval_jaxpr/reduce_sum | solution.py:520
  186.6 3.1 copy-done
  189.6 8.5 %bitcast_dynamic-update-slice_fusion.10 = bf16[2,512,12,64]{1,3,2,0:T(8,128)(2,1)} fusion(bf16[2,512,12,64]{1,3,2,0:T(8,128)(2,1)} %get-tuple-element.583, s32[]{:T(128)S(6)} %copy.90, bf16[1,1024,12,64]{1,3,2,0:T(8,128)(2,1)S(1)} %copy-done.3, f32[12,512,1024]{2,1,0:T(8,128)S(1)} %copy-done, f32[12,512]{1,0:T(8,128)S(1)} %fusion.133, ...), kind=kOutput, calls=%fused_computation.8.clone.1 | convolution fusion | flops 836763648 | bytes 28884996 | tf_op jit(solution)/shard_map/while/body/eval_jaxpr/hqk,khe->qhe/dot_general | solution.py:522
  198.2 3.2 copy.68
  205.3 8.8 %fusion.90 = f32[1024,3072]{1,0:T(8,128)} fusion(bf16[768,3072]{1,0:T(8,128)(2,1)S(1)} %bitcast.201, f32[1024,768]{0,1:T(8,128)S(1)} %get-tuple-element.438, f32[768]{0:T(1024)S(1)} %copy-done.30, f32[768]{0:T(1024)S(1)} %copy-done.29, f32[1024]{0:T(1024)S(1)} %fusion.85, f32[1024]{0:T(1024)S(1)} %broadcast_multiply_fusion), kind=kOutput, calls=%fused_computation.170 | convolution fusion | flops 4835770368 | bytes 20461568 | tf_op jit(solution)/shard_map/dot_general | solution.py:533
  214.2 10.4 %fusion.74 = bf16[1,1024,768]{1,2,0:T(8,128)(2,1)} fusion(f32[1024,768]{0,1:T(8,128)S(1)} %get-tuple-element.438, f32[768]{0:T(1024)S(1)} %copy-done.69, bf16[3072,768]{1,0:T(8,128)(2,1)S(1)} %bitcast.214, f32[1024]{0:T(1024)S(1)} %copy-done.50, f32[1024,3072]{1,0:T(8,128)} %fusion.90, f32[3072]{0:T(1024)S(1)} %copy-done.66), kind=kOutput, calls=%fused_computation.115 | convolution fusion | flops 4866441216 | bytes 22039552 | tf_op jit(solution)/shard_map/dot_general | solution.py:535
  224.6 2.6 copy.76
  227.2 19.7 %convert_reduce_fusion = (f32[3072]{0:T(1024)}, bf16[1024,3072]{1,0:T(8,128)(2,1)S(1)}) fusion(f32[1024,3072]{1,0:T(8,128)} %fusion.90, f32[3072]{0:T(1024)S(1)} %copy-done.66, bf16[3072,768]{1,0:T(8,128)(2,1)} %get-tuple-element.279, bf16[1,1024,768]{1,2,0:T(8,128)(2,1)} %copy.70, f32[1024]{0:T(1024)S(1)} %copy-done.50), kind=kOutput, calls=%fused_computation.63 | convolution fusion | flops 4906546176 | bytes 25194496 | tf_op jit(solution)/shard_map/nd,fd->nf/dot_general | solution.py:544
  246.8 16.1 %convolution_convert_fusion.gd = bf16[3072,768]{1,0:T(8,128)(2,1)} fusion(bf16[1,1024,768]{1,2,0:T(8,128)(2,1)S(1)} %copy-done.13, f32[1024]{0:T(1024)S(1)} %copy-done.50, f32[1024,3072]{1,0:T(8,128)} %fusion.90, f32[3072]{0:T(1024)S(1)} %copy-done.66), kind=kOutput, calls=%fused_computation.65 | convolution fusion | flops 4868014080 | bytes 18890752 | tf_op jit(solution)/shard_map/nf,nd->fd/dot_general | solution.py:540
  262.9 9.8 %fusion.101 = (f32[768]{0:T(1024)}, f32[1024,768]{1,0:T(8,128)}) fusion(bf16[1024,3072]{1,0:T(8,128)(2,1)S(1)} %get-tuple-element.444, bf16[768,3072]{1,0:T(8,128)(2,1)} %get-tuple-element.278), kind=kOutput, calls=%fused_computation.175 | convolution fusion | flops 4832623616 | bytes 14158848 | tf_op jit(solution)/shard_map/nf,df->nd/dot_general | solution.py:553
  272.7 3.5 copy.71
  276.2 4.5 multiply_reduce_fusion.1
  280.7 9.9 %convolution_convert_fusion.1.gu = bf16[768,3072]{1,0:T(8,128)(2,1)} fusion(bf16[1024,3072]{1,0:T(8,128)(2,1)} %copy-done.75, f32[1024,768]{0,1:T(8,128)S(1)} %copy-done.8, f32[768]{0:T(1024)S(1)} %copy-done.30, f32[768]{0:T(1024)S(1)} %copy-done.29, f32[1024]{0:T(1024)S(1)} %fusion.85, f32[1024]{0:T(1024)S(1)} %broadcast_multiply_fusion), kind=kOutput, calls=%fused_computation.66 | convolution fusion | flops 4838129664 | bytes 14170112 | tf_op jit(solution)/shard_map/nd,nf->df/dot_general | solution.py:549
  296.4 2.7 convolution_convert_fusion.3
  300.4 174.3 %while.31 = (s32[]{:T(128)}, bf16[2,512,12,64]{1,3,2,0:T(8,128)(2,1)}, f32[2,1024,12,64]{1,3,2,0:T(8,128)}, f32[2,1024,12,64]{1,3,2,0:T(8,128)}, s32[2]{0:T(128)...) while((s32[]{:T(128)}, ...), condition=%wide.region_12.13_spmd, body=%wide.region_10.12_spmd.sunk | while | flops 4123127296 | bytes 225630672 | solution.py:595
  305.6 11.4 %fusion.142 = f32[12,512,1024]{2,1,0:T(8,128)} fusion(bf16[1,1024,12,64]{1,3,2,0:T(8,128)(2,1)S(1)} %get-tuple-element.647, bf16[1,1024,12,64]{1,3,2,0:T(8,128)(2,1)} %copy-done.1, s32[]{:T(128)S(6)} %select_n.110), kind=kOutput, calls=%fused_computation.35.clone.1 | convolution fusion | flops 805306368 | bytes 27525124 | tf_op jit(solution)/shard_map/while/body/eval_jaxpr/qhe,khe->hqk/dot_general | solution.py:500
  317.0 13.1 %bitcast_dynamic-update-slice_fusion.14 = f32[2,1024,12,64]{1,3,2,0:T(8,128)} fusion(f32[2,1024,12,64]{1,3,2,0:T(8,128)} %get-tuple-element.627, s32[]{:T(128)S(6)} %copy.100, f32[12,512,1024]{2,1,0:T(8,128)} %fusion.142, f32[12,512]{1,0:T(8,128)S(1)} %dynamic-slice_bitcast_fusion.2, pred[512,1024]{1,0:T(8,128)(4,1)S(1)} %fusion.143, ...), kind=kOutput, calls=%fused_computation.26.clone.1 | convolution fusion | flops 830472192 | bytes 29655048 | tf_op jit(solution)/shard_map/while/body/eval_jaxpr/hqk,qhe->khe/dot_general | solution.py:590
  330.1 18.1 %multiply_reduce_fusion.10 = (f32[12,512]{1,0:T(8,128)S(1)}, f32[12,512,1024]{2,1,0:T(8,128)}) fusion(f32[12,512,1024]{2,1,0:T(8,128)} %fusion.142, f32[12,512]{1,0:T(8,128)S(1)} %dynamic-slice_bitcast_fusion.2, pred[512,1024]{1,0:T(8,128)(4,1)S(1)} %fusion.143, bf16[1,1024,12,64]{1,3,2,0:T(8,128)(2,1)} %get-tuple-element.650, ...), kind=kOutput, calls=%fused_computation.21.clone.1 | convolution fusion | flops 836757504 | bytes 53264388 | tf_op jit(solution)/shard_map/while/body/eval_jaxpr/qhe,khe->hqk/dot_general | solution.py:577
  348.2 21.2 %multiply_convert_fusion.6 = bf16[12,512,1024]{2,1,0:T(8,128)(2,1)} fusion(f32[12,512,1024]{2,1,0:T(8,128)} %get-tuple-element.567, f32[12,512,1024]{2,1,0:T(8,128)} %fusion.142, f32[12,512]{1,0:T(8,128)S(1)} %get-tuple-element.568, f32[12,512]{1,0:T(8,128)S(1)} %dynamic-slice_bitcast_fusion.2, pred[512,1024]{1,0:T(8,128)(4,1)S(1)} %fusion.143), kind=kLoop, calls=%fused_computation.20.clone.1 | loop fusion | flops 37748736 | bytes 63488000 | tf_op jit(solution)/shard_map/while/body/eval_jaxpr/convert_element_type | solution.py:581
  369.5 9.5 %bitcast_dynamic-update-slice_fusion.12 = bf16[2,512,12,64]{1,3,2,0:T(8,128)(2,1)} fusion(bf16[2,512,12,64]{1,3,2,0:T(8,128)(2,1)} %get-tuple-element.625, s32[]{:T(128)S(6)} %copy.100, bf16[12,512,1024]{2,1,0:T(8,128)(2,1)} %multiply_convert_fusion.6, bf16[1,1024,12,64]{1,3,2,0:T(8,128)(2,1)S(1)} %get-tuple-element.647), kind=kOutput, calls=%fused_computation.30.clone.1 | convolution fusion | flops 805699584 | bytes 15728644 | tf_op jit(solution)/shard_map/while/body/eval_jaxpr/hqk,khe->qhe/dot_general | solution.py:583
  379.0 8.5 %bitcast_dynamic-update-slice_fusion.13 = f32[2,1024,12,64]{1,3,2,0:T(8,128)} fusion(f32[2,1024,12,64]{1,3,2,0:T(8,128)} %get-tuple-element.626, s32[]{:T(128)S(6)} %copy.100, bf16[12,512,1024]{2,1,0:T(8,128)(2,1)} %multiply_convert_fusion.6, bf16[1,1024,12,64]{1,3,2,0:T(8,128)(2,1)S(1)} %copy-done.2, s32[]{:T(128)S(6)} %select_n.110), kind=kOutput, calls=%fused_computation.27.clone.1 | convolution fusion | flops 806092800 | bytes 16515080 | tf_op jit(solution)/shard_map/while/body/eval_jaxpr/hqk,qhe->khe/dot_general | solution.py:587
  392.5 11.4 %fusion.142 = f32[12,512,1024]{2,1,0:T(8,128)} fusion(bf16[1,1024,12,64]{1,3,2,0:T(8,128)(2,1)S(1)} %get-tuple-element.647, bf16[1,1024,12,64]{1,3,2,0:T(8,128)(2,1)} %copy-done.1, s32[]{:T(128)S(6)} %select_n.110), kind=kOutput, calls=%fused_computation.35.clone.1 | convolution fusion | flops 805306368 | bytes 27525124 | tf_op jit(solution)/shard_map/while/body/eval_jaxpr/qhe,khe->hqk/dot_general | solution.py:500
  403.9 13.0 %bitcast_dynamic-update-slice_fusion.14 = f32[2,1024,12,64]{1,3,2,0:T(8,128)} fusion(f32[2,1024,12,64]{1,3,2,0:T(8,128)} %get-tuple-element.627, s32[]{:T(128)S(6)} %copy.100, f32[12,512,1024]{2,1,0:T(8,128)} %fusion.142, f32[12,512]{1,0:T(8,128)S(1)} %dynamic-slice_bitcast_fusion.2, pred[512,1024]{1,0:T(8,128)(4,1)S(1)} %fusion.143, ...), kind=kOutput, calls=%fused_computation.26.clone.1 | convolution fusion | flops 830472192 | bytes 29655048 | tf_op jit(solution)/shard_map/while/body/eval_jaxpr/hqk,qhe->khe/dot_general | solution.py:590
  416.9 18.1 %multiply_reduce_fusion.10 = (f32[12,512]{1,0:T(8,128)S(1)}, f32[12,512,1024]{2,1,0:T(8,128)}) fusion(f32[12,512,1024]{2,1,0:T(8,128)} %fusion.142, f32[12,512]{1,0:T(8,128)S(1)} %dynamic-slice_bitcast_fusion.2, pred[512,1024]{1,0:T(8,128)(4,1)S(1)} %fusion.143, bf16[1,1024,12,64]{1,3,2,0:T(8,128)(2,1)} %get-tuple-element.650, ...), kind=kOutput, calls=%fused_computation.21.clone.1 | convolution fusion | flops 836757504 | bytes 53264388 | tf_op jit(solution)/shard_map/while/body/eval_jaxpr/qhe,khe->hqk/dot_general | solution.py:577
  435.0 21.2 %multiply_convert_fusion.6 = bf16[12,512,1024]{2,1,0:T(8,128)(2,1)} fusion(f32[12,512,1024]{2,1,0:T(8,128)} %get-tuple-element.567, f32[12,512,1024]{2,1,0:T(8,128)} %fusion.142, f32[12,512]{1,0:T(8,128)S(1)} %get-tuple-element.568, f32[12,512]{1,0:T(8,128)S(1)} %dynamic-slice_bitcast_fusion.2, pred[512,1024]{1,0:T(8,128)(4,1)S(1)} %fusion.143), kind=kLoop, calls=%fused_computation.20.clone.1 | loop fusion | flops 37748736 | bytes 63488000 | tf_op jit(solution)/shard_map/while/body/eval_jaxpr/convert_element_type | solution.py:581
  456.3 9.5 %bitcast_dynamic-update-slice_fusion.12 = bf16[2,512,12,64]{1,3,2,0:T(8,128)(2,1)} fusion(bf16[2,512,12,64]{1,3,2,0:T(8,128)(2,1)} %get-tuple-element.625, s32[]{:T(128)S(6)} %copy.100, bf16[12,512,1024]{2,1,0:T(8,128)(2,1)} %multiply_convert_fusion.6, bf16[1,1024,12,64]{1,3,2,0:T(8,128)(2,1)S(1)} %get-tuple-element.647), kind=kOutput, calls=%fused_computation.30.clone.1 | convolution fusion | flops 805699584 | bytes 15728644 | tf_op jit(solution)/shard_map/while/body/eval_jaxpr/hqk,khe->qhe/dot_general | solution.py:583
  465.8 8.6 %bitcast_dynamic-update-slice_fusion.13 = f32[2,1024,12,64]{1,3,2,0:T(8,128)} fusion(f32[2,1024,12,64]{1,3,2,0:T(8,128)} %get-tuple-element.626, s32[]{:T(128)S(6)} %copy.100, bf16[12,512,1024]{2,1,0:T(8,128)(2,1)} %multiply_convert_fusion.6, bf16[1,1024,12,64]{1,3,2,0:T(8,128)(2,1)S(1)} %copy-done.2, s32[]{:T(128)S(6)} %select_n.110), kind=kOutput, calls=%fused_computation.27.clone.1 | convolution fusion | flops 806092800 | bytes 16515080 | tf_op jit(solution)/shard_map/while/body/eval_jaxpr/hqk,qhe->khe/dot_general | solution.py:587
  474.7 3.9 reduce_sum.262
  484.5 5.2 reduce_sum.261
  489.7 7.8 %fusion.100 = (f32[768]{0:T(1024)S(1)}, f32[1024,768]{1,0:T(8,128)}) fusion(bf16[768,2048]{1,0:T(8,128)(2,1)} %get-tuple-element.275, bf16[1024,384]{0,1:T(8,128)(2,1)} %bitcast.211, bf16[1024,768]{0,1:T(8,128)(2,1)} %bitcast.209, bf16[1024,768]{0,1:T(8,128)(2,1)S(1)} %bitcast.207), kind=kOutput, calls=%fused_computation.174 | convolution fusion | flops 3032481024 | bytes 10030080 | tf_op jit(solution)/shard_map/ne,de->nd/dot_general | solution.py:614
  497.6 3.6 convolution_convert_fusion.2
  503.3 92.0 %shard_map.416 = (f32[24,2048]{1,0:T(8,128)}, f32[24,768]{1,0:T(8,128)}, f32[24,3072]{1,0:T(8,128)}, f32[96,768]{1,0:T(8,128)}, f32[8,128]{1,0:T(8,128)}) custom-call(bf16[768,2048]{1,0:T(8,128)(2,1)} %pad.4.gi, bf16[768,768]{1,0:T(8,128)(2,1)} %convolution_convert_fusion.4.go, bf16[768,3072]{1,0:T(8,128)(2,1)} %convolution_convert_fusion.1.gu, ...), custom_call_target="tpu_custom_call" | custom-call | tf_op jit(solution)/shard_map/pallas_call | solution.py:349
  604.3 3.6 copy.73
  607.9 2.6 fusion.62
  612.2 40.3 %all-reduce.1 = (f32[]{:T(128)}, f32[8832]{0:T(1024)S(1)}) all-reduce(f32[]{:T(128)S(6)} %add.338, f32[8832]{0:T(1024)S(1)} %constant_dynamic-update-slice_fusion), channel_id=1, replica_groups=mesh['wide'=8,'narrow'=4] {'wide','narrow'}, use_global_device_ids=true, to_apply=%region_21.22 | all-reduce | flops 8833 | bytes 70664 | tf_op jit(solution)/shard_map/psum | solution.py:645
  654.6 5.6 fusion.72
  660.3 2.8 copy.77
  (254 shorter events, 55.2 us)
Async XLA Ops:
  5.8 96.1 %copy-start.48 = (f32[768]{0:T(1024)}, f32[768]{0:T(1024)S(1)}, u32[]{:S(2)}) copy-start(f32[768]{0:T(1024)S(1)} %get-tuple-element.435) | copy-start | bytes 9220
  5.8 96.1 %copy-start.67 = (f32[768]{0:T(1024)}, f32[768]{0:T(1024)S(1)}, u32[]{:S(2)}) copy-start(f32[768]{0:T(1024)S(1)} %get-tuple-element.434) | copy-start | bytes 9220
  9.0 92.9 %copy-start.4 = (bf16[1,1024,768]{1,2,0:T(8,128)(2,1)}, bf16[1,1024,768]{1,2,0:T(8,128)(2,1)S(1)}, u32[]{:S(2)}) copy-start(bf16[1,1024,768]{1,2,0:T(8,128)(2,1)S(1)} %copy.63) | copy-start | bytes 4718596
  9.3 98.2 %copy-start.43 = (f32[1024]{0:T(1024)}, f32[1024]{0:T(1024)S(1)}, u32[]{:S(2)}) copy-start(f32[1024]{0:T(1024)S(1)} %broadcast_multiply_fusion.1) | copy-start | bytes 12292
  9.8 97.7 %copy-start.56 = (f32[1024]{0:T(1024)}, f32[1024]{0:T(1024)S(1)}, u32[]{:S(2)}) copy-start(f32[1024]{0:T(1024)S(1)} %fusion.61) | copy-start | bytes 12292
  9.8 97.7 %copy-start.52 = (f32[1024]{0:T(1024)}, f32[1024]{0:T(1024)S(1)}, u32[]{:S(2)}) copy-start(f32[1024]{0:T(1024)S(1)} %fusion.84) | copy-start | bytes 12292
  125.4 22.9 %copy-start.3 = (bf16[1,1024,12,64]{1,3,2,0:T(8,128)(2,1)S(1)}, bf16[1,1024,12,64]{1,3,2,0:T(8,128)(2,1)}, u32[]{:S(2)}) copy-start(bf16[1,1024,12,64]{1,3,2,0:T(8,128)(2,1)} %get-tuple-element.602) | copy-start | bytes 4718596 | tf_op jit(solution)/shard_map/while
  136.1 15.4 %copy-start = (f32[12,512,1024]{2,1,0:T(8,128)S(1)}, f32[12,512,1024]{2,1,0:T(8,128)}, u32[]{:S(2)}) copy-start(f32[12,512,1024]{2,1,0:T(8,128)} %get-tuple-element.554) | copy-start | bytes 75497472 | tf_op jit(solution)/shard_map/while
  163.6 22.9 %copy-start.3 = (bf16[1,1024,12,64]{1,3,2,0:T(8,128)(2,1)S(1)}, bf16[1,1024,12,64]{1,3,2,0:T(8,128)(2,1)}, u32[]{:S(2)}) copy-start(bf16[1,1024,12,64]{1,3,2,0:T(8,128)(2,1)} %get-tuple-element.602) | copy-start | bytes 4718596 | tf_op jit(solution)/shard_map/while
  174.3 15.4 %copy-start = (f32[12,512,1024]{2,1,0:T(8,128)S(1)}, f32[12,512,1024]{2,1,0:T(8,128)}, u32[]{:S(2)}) copy-start(f32[12,512,1024]{2,1,0:T(8,128)} %get-tuple-element.554) | copy-start | bytes 75497472 | tf_op jit(solution)/shard_map/while
  203.5 10.6 %copy-start.7 = (f32[1024,768]{0,1:T(8,128)}, f32[1024,768]{0,1:T(8,128)S(1)}, u32[]{:S(2)}) copy-start(f32[1024,768]{0,1:T(8,128)S(1)} %get-tuple-element.438) | copy-start | bytes 9437188
  203.6 10.5 %slice-start.2 = ((s8[4718592]{0:T(1024)(128)(4,1)}), s8[4194304]{0:T(1024)(128)(4,1)S(1)}, s32[]{:S(2)}) async-start(s8[4718592]{0:T(1024)(128)(4,1)} %bitcast.213), calls=%async_computation.2 | async-start | bytes 8388608
  205.3 8.8 %copy-start.50 = (f32[1024]{0:T(1024)S(1)}, f32[1024]{0:T(1024)}, u32[]{:S(2)}) copy-start(f32[1024]{0:T(1024)} %fusion.83) | copy-start | bytes 12292
  205.3 8.8 %copy-start.66 = (f32[3072]{0:T(1024)S(1)}, f32[3072]{0:T(1024)}, u32[]{:S(2)}) copy-start(f32[3072]{0:T(1024)} %slice.61) | copy-start | bytes 36868
  205.3 8.8 %copy-start.69 = (f32[768]{0:T(1024)S(1)}, f32[768]{0:T(1024)}, u32[]{:S(2)}) copy-start(f32[768]{0:T(1024)} %get-tuple-element.436) | copy-start | bytes 9220
  205.3 8.8 %slice-start.3 = ((s8[4718592]{0:T(1024)(128)(4,1)}), s8[524288]{0:T(1024)(128)(4,1)S(1)}, s32[]{:S(2)}) async-start(s8[4718592]{0:T(1024)(128)(4,1)} %bitcast.213), calls=%async_computation.3 | async-start | bytes 1048576
  227.2 19.7 %copy-start.13 = (bf16[1,1024,768]{1,2,0:T(8,128)(2,1)S(1)}, bf16[1,1024,768]{1,2,0:T(8,128)(2,1)}, u32[]{:S(2)}) copy-start(bf16[1,1024,768]{1,2,0:T(8,128)(2,1)} %copy.70) | copy-start | bytes 4718596
  246.8 16.1 %copy-start.75 = (bf16[1024,3072]{1,0:T(8,128)(2,1)}, bf16[1024,3072]{1,0:T(8,128)(2,1)S(1)}, u32[]{:S(2)}) copy-start(bf16[1024,3072]{1,0:T(8,128)(2,1)S(1)} %get-tuple-element.444) | copy-start | bytes 18874372
  276.2 4.5 copy-start.8
  280.7 9.9 %copy-start.11 = (f32[1024,768]{0,1:T(8,128)S(1)}, f32[1024,768]{0,1:T(8,128)}, u32[]{:S(2)}) copy-start(f32[1024,768]{0,1:T(8,128)} %copy.71) | copy-start | bytes 9437188
  296.4 4.0 copy-start.74
  300.6 4.6 copy-start.1
  305.6 11.4 %copy-start.16 = (bf16[1,1024,12,64]{1,3,2,0:T(8,128)(2,1)S(1)}, bf16[1,1024,12,64]{1,3,2,0:T(8,128)(2,1)}, u32[]{:S(2)}) copy-start(bf16[1,1024,12,64]{1,3,2,0:T(8,128)(2,1)} %get-tuple-element.649) | copy-start | bytes 4718596 | tf_op jit(solution)/shard_map/while
  369.5 9.5 %copy-start.2 = (bf16[1,1024,12,64]{1,3,2,0:T(8,128)(2,1)S(1)}, bf16[1,1024,12,64]{1,3,2,0:T(8,128)(2,1)}, u32[]{:S(2)}) copy-start(bf16[1,1024,12,64]{1,3,2,0:T(8,128)(2,1)} %copy-done.1) | copy-start | bytes 4718596 | tf_op jit(solution)/shard_map/while
  387.5 4.6 copy-start.1
  392.5 11.4 %copy-start.16 = (bf16[1,1024,12,64]{1,3,2,0:T(8,128)(2,1)S(1)}, bf16[1,1024,12,64]{1,3,2,0:T(8,128)(2,1)}, u32[]{:S(2)}) copy-start(bf16[1,1024,12,64]{1,3,2,0:T(8,128)(2,1)} %get-tuple-element.649) | copy-start | bytes 4718596 | tf_op jit(solution)/shard_map/while
  456.3 9.5 %copy-start.2 = (bf16[1,1024,12,64]{1,3,2,0:T(8,128)(2,1)S(1)}, bf16[1,1024,12,64]{1,3,2,0:T(8,128)(2,1)}, u32[]{:S(2)}) copy-start(bf16[1,1024,12,64]{1,3,2,0:T(8,128)(2,1)} %copy-done.1) | copy-start | bytes 4718596 | tf_op jit(solution)/shard_map/while
  484.5 5.2 copy-start.20
  489.7 7.9 %copy-start.6 = (bf16[1,1024,768]{1,2,0:T(8,128)(2,1)S(1)}, bf16[1,1024,768]{1,2,0:T(8,128)(2,1)}, u32[]{:S(2)}) copy-start(bf16[1,1024,768]{1,2,0:T(8,128)(2,1)} %copy-done.4) | copy-start | bytes 4718596
  489.7 7.9 %copy-start.21 = (bf16[1024,12,64]{0,2,1:T(8,128)(2,1)S(1)}, bf16[1024,12,64]{0,2,1:T(8,128)(2,1)}, u32[]{:S(2)}) copy-start(bf16[1024,12,64]{0,2,1:T(8,128)(2,1)} %reduce_sum.261) | copy-start | bytes 4718596
  489.7 7.9 %copy-start.26 = (bf16[1,1024,6,64]{1,3,2,0:T(8,128)(2,1)S(1)}, bf16[1,1024,6,64]{1,3,2,0:T(8,128)(2,1)}, u32[]{:S(2)}) copy-start(bf16[1,1024,6,64]{1,3,2,0:T(8,128)(2,1)} %get-tuple-element.422) | copy-start | bytes 2359300
  489.7 7.9 %copy-start.44 = (f32[1024]{0:T(1024)S(1)}, f32[1024]{0:T(1024)}, u32[]{:S(2)}) copy-start(f32[1024]{0:T(1024)} %copy-done.43) | copy-start | bytes 12292
  489.7 7.9 %copy-start.49 = (f32[768]{0:T(1024)S(1)}, f32[768]{0:T(1024)}, u32[]{:S(2)}) copy-start(f32[768]{0:T(1024)} %copy-done.48) | copy-start | bytes 9220
  489.7 7.9 %copy-start.53 = (f32[1024]{0:T(1024)S(1)}, f32[1024]{0:T(1024)}, u32[]{:S(2)}) copy-start(f32[1024]{0:T(1024)} %copy-done.52) | copy-start | bytes 12292
  489.7 7.9 %copy-start.68 = (f32[768]{0:T(1024)S(1)}, f32[768]{0:T(1024)}, u32[]{:S(2)}) copy-start(f32[768]{0:T(1024)} %copy-done.67) | copy-start | bytes 9220
  610.5 44.0 %copy-start.15 = (bf16[1,1024,768]{1,2,0:T(8,128)(2,1)S(1)}, bf16[1,1024,768]{1,2,0:T(8,128)(2,1)}, u32[]{:S(2)}) copy-start(bf16[1,1024,768]{1,2,0:T(8,128)(2,1)} %copy.70) | copy-start | bytes 4718596
  610.5 44.0 %copy-start.51 = (f32[1024]{0:T(1024)S(1)}, f32[1024]{0:T(1024)}, u32[]{:S(2)}) copy-start(f32[1024]{0:T(1024)} %fusion.83) | copy-start | bytes 12292
  610.6 44.0 %copy-start.55 = (f32[1024]{0:T(1024)S(1)}, f32[1024]{0:T(1024)}, u32[]{:S(2)}) copy-start(f32[1024]{0:T(1024)} %copy-done.54) | copy-start | bytes 12292
  660.2 4.4 copy-start.27
  660.2 4.4 copy-start.28
  660.2 4.4 copy-start.39
  660.2 4.4 copy-start.40
  660.3 4.4 copy-start.41
  660.3 5.4 copy-start.22
  660.3 5.4 copy-start.25
  660.3 5.4 copy-start.33
  660.3 5.4 copy-start.34
  660.3 5.4 copy-start.35
  (37 other events, 103.1 us)
